TPU v7x, 256 devices: a whole 4x4x8 slice. The times are simulated.
256 devices in a mesh: dp: 16 (over x_lo, y, core), ctx: 16 (over x_hi, z).
Axes of the slice: x: 4 (x_hi: 2, x_lo: 2; x = x_hi * 2 + x_lo), y: 4, z: 8, core: 2. Of those that a mesh axis runs over, the one named last changes fastest.
Arguments:
- q_latent: bfloat16 [16, 2048, 32768], P('dp', 'ctx'), may hold values from -15 to 15
- q_rope: bfloat16 [16, 2048, 4096], P('dp', 'ctx'), may hold values from -4 to 4
- latent_cache: bfloat16 [16, 3072, 512], P('dp', 'ctx'), may hold values from -4 to 4
- rope_keys: bfloat16 [16, 3072, 64], P('dp', 'ctx'), may hold values from -4 to 4
- up_weight: bfloat16 [64, 512, 128], P('ctx', 'dp'), may hold values from -0.25 to 0.25
- out_grad: bfloat16 [16, 2048, 8192], P('dp', 'ctx'), may hold values from -6 to 6
- block_ids: int32 [16, 32, 4], P('dp', 'ctx'), may hold values from 0 to 47, as said below
- block_counts: int32 [16, 32], P('dp', 'ctx'), may hold values from 1 to 4, as said below
- slab_offset: int32 [16], P('dp'), may hold values from 0 to 1024, as said below
Outputs:
- cache_grad: bfloat16 [16, 3072, 512], P('dp', 'ctx')
- rope_grad: bfloat16 [16, 3072, 64], P('dp', 'ctx')
- weight_grad: float32 [64, 512, 128], P('ctx', 'dp')
Inputs may be any that keep to these rules, and one draw needn't show every extreme that they name: `slab_offset`: A multiple of 64; the queries lie inside the context. `block_ids`: for query block b of a sequence with offset o, entry 0 is the key block o / 64 + b; entries 1 to count - 1 are distinct key blocks before it; entries from count on repeat entry 0. `block_counts`: count = 1 + min(3, o / 64 + b) for query block b of a sequence with offset o.
All inputs are finite; a program needn't handle non-finite values.
Results may differ from a plain program's by a relative error of at most 0.022.
Values may be sent and summed in bfloat16 or wider, within the bound.
A program may use at most 192 MiB of HBM per device.

v0:
```python
import jax
import jax.numpy as jnp
from jax import lax
from jax.sharding import PartitionSpec as P

LAT = 512
ROPE = 64
HD = 128
BLK = 64
SEL = 4


def key_rows(block_list):
    within = jnp.arange(BLK, dtype=jnp.int32)
    return (block_list[:, :, None] * BLK + within[None, None, :]).reshape(
        block_list.shape[0], SEL * BLK
    )


def attend(q_lat, q_rot, block_list, block_valid, first_block, offset, cache_full, rope_full):
    block_count = block_list.shape[0]
    head_count = q_lat.shape[1] // LAT
    score_scale = (HD + ROPE) ** (-0.5)
    key_index = key_rows(block_list)
    key_tiles = jnp.take(cache_full, key_index, axis=0)
    rope_tiles = jnp.take(rope_full, key_index, axis=0)
    q_tiles = q_lat.reshape(block_count, BLK, head_count, LAT)
    qrope_tiles = q_rot.reshape(block_count, BLK, head_count, ROPE)
    scores = jnp.einsum("bthl,bkl->bthk", q_tiles, key_tiles, preferred_element_type=jnp.float32)
    scores = (
        scores
        + jnp.einsum("bthr,bkr->bthk", qrope_tiles, rope_tiles, preferred_element_type=jnp.float32)
    ) * score_scale
    query_block = first_block + jnp.arange(block_count, dtype=jnp.int32)
    positions = offset + query_block[:, None] * BLK + jnp.arange(BLK, dtype=jnp.int32)[None, :]
    slot_index = jnp.arange(SEL * BLK, dtype=jnp.int32) // BLK
    visible = (slot_index[None, None, :] < block_valid[:, None, None]) & (
        key_index[:, None, :] <= positions[:, :, None]
    )
    scores = jnp.where(visible[:, :, None, :], scores, -1e30)
    row_top = jnp.max(scores, axis=-1, keepdims=True)
    raw_weights = jnp.exp(scores - row_top)
    attention = raw_weights / jnp.sum(raw_weights, axis=-1, keepdims=True)
    attn_half = attention.astype(jnp.bfloat16)
    out_latent = jnp.einsum(
        "bthk,bkl->bthl", attn_half, key_tiles, preferred_element_type=jnp.float32
    ).astype(jnp.bfloat16)
    stored = (attention, attn_half, key_tiles, q_tiles, qrope_tiles)
    return (stored, out_latent.reshape(block_count * BLK, head_count * LAT))


def project(out_latent, grad_out, weight):
    head_count = weight.shape[0]
    latent_rows = out_latent.reshape(-1, head_count, LAT)
    grad_rows = grad_out.reshape(-1, head_count, HD)
    weight_part = jnp.einsum(
        "thl,thd->hld", latent_rows, grad_rows, preferred_element_type=jnp.float32
    )
    latent_back = jnp.einsum(
        "thd,hld->thl", grad_rows, weight, preferred_element_type=jnp.float32
    ).astype(jnp.bfloat16)
    return (weight_part, latent_back.reshape(latent_rows.shape[0], head_count * LAT))


def attend_back(stored, block_list, latent_back, key_blocks):
    attention, attn_half, key_tiles, q_tiles, qrope_tiles = stored
    block_count = block_list.shape[0]
    head_count = q_tiles.shape[2]
    score_scale = (HD + ROPE) ** (-0.5)
    grad_latent = latent_back.reshape(block_count, BLK, head_count, LAT)
    prob_back = jnp.einsum(
        "bthl,bkl->bthk", grad_latent, key_tiles, preferred_element_type=jnp.float32
    )
    row_delta = jnp.sum(attention * prob_back, axis=-1, keepdims=True)
    score_back = (attention * (prob_back - row_delta)).astype(jnp.bfloat16)
    grad_key = jnp.einsum(
        "bthk,bthl->bkl", attn_half, grad_latent, preferred_element_type=jnp.float32
    )
    grad_key = grad_key + score_scale * jnp.einsum(
        "bthk,bthl->bkl", score_back, q_tiles, preferred_element_type=jnp.float32
    )
    grad_rope = score_scale * jnp.einsum(
        "bthk,bthr->bkr", score_back, qrope_tiles, preferred_element_type=jnp.float32
    )
    flat_rows = key_rows(block_list).reshape(-1)
    dense_key = (
        jnp.zeros((key_blocks * BLK, LAT), jnp.float32).at[flat_rows].add(grad_key.reshape(-1, LAT))
    )
    dense_rope = (
        jnp.zeros((key_blocks * BLK, ROPE), jnp.float32)
        .at[flat_rows]
        .add(grad_rope.reshape(-1, ROPE))
    )
    return (dense_key, dense_rope)


def shards(
    q_latent,
    q_rope,
    latent_cache,
    rope_keys,
    up_weight,
    out_grad,
    block_ids,
    block_counts,
    slab_offset,
):
    offset = slab_offset[0]
    cache_full, rope_full = (
        lax.all_gather(latent_cache[0], "ctx", axis=0, tiled=True),
        lax.all_gather(rope_keys[0], "ctx", axis=0, tiled=True),
    )
    weight = lax.all_gather(up_weight, "dp", axis=1, tiled=True)
    key_blocks = cache_full.shape[0] // BLK
    block_list = block_ids[0]
    block_valid = block_counts[0]
    first_block = lax.axis_index("ctx") * block_list.shape[0]
    stored, out_latent = attend(
        q_latent[0], q_rope[0], block_list, block_valid, first_block, offset, cache_full, rope_full
    )
    head_latent, head_grad = (
        lax.all_to_all(out_latent, "ctx", split_axis=1, concat_axis=0, tiled=True),
        lax.all_to_all(out_grad[0], "ctx", split_axis=1, concat_axis=0, tiled=True),
    )
    weight_part, back_heads = project(head_latent, head_grad, weight)
    latent_back = lax.all_to_all(back_heads, "ctx", split_axis=0, concat_axis=1, tiled=True)
    dense_key, dense_rope = attend_back(stored, block_list, latent_back, key_blocks)
    weight_grad = lax.psum_scatter(
        weight_part.astype(jnp.bfloat16), "dp", scatter_dimension=1, tiled=True
    ).astype(jnp.float32)
    cache_share, rope_share = (
        lax.psum_scatter(dense_key, "ctx", scatter_dimension=0, tiled=True),
        lax.psum_scatter(dense_rope, "ctx", scatter_dimension=0, tiled=True),
    )
    return (
        cache_share.astype(jnp.bfloat16)[None],
        rope_share.astype(jnp.bfloat16)[None],
        weight_grad,
    )


def solution(mesh):
    placed = (
        P("dp", "ctx", None),
        P("dp", "ctx", None),
        P("dp", "ctx", None),
        P("dp", "ctx", None),
        P("ctx", "dp", None),
        P("dp", "ctx", None),
        P("dp", "ctx", None),
        P("dp", "ctx"),
        P("dp"),
    )
    return jax.shard_map(
        shards,
        mesh=mesh,
        in_specs=placed,
        out_specs=(P("dp", "ctx", None), P("dp", "ctx", None), P("ctx", "dp", None)),
        check_vma=False,
    )
```

profile of v0, /device:TPU:8, one launch (start us, length us, event | category | flops | bytes accessed | tf_op | source)
XLA Modules:
  0.0 1031.4 jit_solution(15219790898963613691)
XLA Ops:
  7.2 4.1 copy.39
  11.2 11.0 %all-to-all-start = ((bf16[128,16,512]{0,2,1:T(8,128)(2,1)}), bf16[128,16,512]{0,2,1:T(8,128)(2,1)S(1)}, u32[]{:S(2)}, u32[]{:S(2)}) async-start(bf16[128,16,512]{0,2,1:T(8,128)(2,1)} %bitcast.102), calls=%async_computation | async-start | bytes 4194304 | tf_op jit(solution)/shard_map/all_to_all | solution.py:123
  22.3 19.2 %all_gather.11 = bf16[4,512,128]{2,1,0:T(8,128)(2,1)S(1)} all-gather(bf16[4,32,128]{2,1,0:T(8,128)(2,1)S(1)} %copy-done.4), channel_id=1, replica_groups=mesh['dp'=16,'ctx'=16] {'dp'}, dimensions={1}, use_global_device_ids=true | all-gather | bytes 557056 | tf_op jit(solution)/shard_map/all_gather | solution.py:113
  41.5 31.2 %all-to-all-done = bf16[128,16,512]{0,2,1:T(8,128)(2,1)S(1)} async-done(((bf16[128,16,512]{0,2,1:T(8,128)(2,1)}), bf16[128,16,512]{0,2,1:T(8,128)(2,1)S(1)}, u32[]{:S(2)}, u32[]{:S(2)}) %all-to-all-start) | async-done | bytes 2097184 | tf_op jit(solution)/shard_map/all_to_all | solution.py:123
  72.8 2.7 copy.40
  75.5 2.8 reshape.230
  78.3 5.6 convolution_convert_fusion.1
  83.9 9.8 copy.64
  93.6 12.5 %copy.42 = bf16[16,128,2048]{2,1,0:T(8,128)(2,1)} copy(bf16[16,128,2048]{1,0,2:T(8,128)(2,1)} %bitcast.99) | data formatting | bytes 16777216 | tf_op jit(solution)/shard_map/all_to_all | solution.py:126
  106.2 5.8 all-to-all-start.1
  112.0 0.0 all-gather.4.cloned.1.call-start
  112.0 0.7 all-gather.4.cloned.1.call-update
  112.8 0.1 add.161
  112.8 0.1 add.166
  112.9 0.1 add.180
  113.0 0.1 add.168
  113.1 0.0 copy-start.7
  113.1 10.2 copy.63
  123.3 0.1 copy.37
  123.5 230.5 %all-gather.1 = bf16[1,3072,64]{2,1,0:T(8,128)(2,1)S(1)} all-gather(bf16[1,192,64]{2,1,0:T(8,128)(2,1)S(1)} %copy.37), channel_id=3, replica_groups=mesh['dp'=16,'ctx'=16] {'ctx'}, dimensions={1}, use_global_device_ids=true | all-gather | bytes 417792 | tf_op jit(solution)/shard_map/all_gather | solution.py:111
  353.9 1.3 gather_fusion.1
  355.3 0.1 copy.38
  356.0 2.3 reshape_squeeze.7
  358.4 0.1 iota_add_fusion.1
  358.4 0.1 broadcast_compare_fusion
  358.5 0.1 compare_and_fusion
  358.6 0.0 all-gather.4.cloned.1.call-done
  358.7 4.3 gather_fusion
  362.9 9.0 fusion.3
  372.0 7.5 fusion.46
  379.5 6.8 convolution_convert_fusion
  386.4 14.1 %all_to_all.42 = bf16[128,16,2048]{2,1,0:T(8,128)(2,1)} reshape(bf16[2,64,64,512]{3,2,1,0:T(8,128)(2,1)} %convolution_convert_fusion) | data formatting | bytes 16777216 | tf_op jit(solution)/shard_map/all_to_all | solution.py:122
  400.5 11.2 %copy.47 = bf16[128,16,2048]{2,0,1:T(8,128)(2,1)} copy(bf16[128,16,2048]{2,1,0:T(8,128)(2,1)} %all_to_all.42) | data formatting | bytes 16777216 | tf_op jit(solution)/shard_map/all_to_all | solution.py:122
  411.7 0.0 all-to-all-done.1
  411.7 6.8 all-to-all-start.2
  418.5 0.0 reduce-scatter.6.cloned.1.call-start
  418.5 0.1 iota_add_fusion
  418.6 0.1 add.164
  418.7 11.2 %copy.43 = bf16[128,16,2048]{2,1,0:T(8,128)(2,1)} copy(bf16[128,16,2048]{2,0,1:T(8,128)(2,1)} %bitcast.16) | data formatting | bytes 16777216 | tf_op jit(solution)/shard_map/all_to_all | solution.py:126
  429.9 14.3 %reshape.231 = bf16[2,64,64,512]{3,2,1,0:T(8,128)(2,1)} reshape(bf16[128,16,2048]{2,1,0:T(8,128)(2,1)} %copy.43) | data formatting | bytes 16777216 | tf_op jit(solution)/shard_map/reshape | solution.py:70
  444.2 7.3 multiply_reduce_fusion
  451.6 6.1 multiply_convert_fusion
  457.7 1.9 copy-done
  459.6 1.0 fusion.27
  460.7 0.1 copy.59
  460.8 3.5 scatter_custom_fusion.1
  464.3 0.0 reduce-scatter.6.cloned.1.call-update
  464.3 0.0 reduce-scatter.8.cloned.1.call-start
  464.3 8.0 fusion.21
  472.3 133.2 %all-to-all-done.2 = bf16[128,16,2048]{2,0,1:T(8,128)(2,1)} async-done(((bf16[128,16,2048]{2,0,1:T(8,128)(2,1)}), bf16[128,16,2048]{2,0,1:T(8,128)(2,1)}, u32[]{:S(2)}, u32[]{:S(2)}) %all-to-all-start.2) | async-done | bytes 8388640 | tf_op jit(solution)/shard_map/all_to_all | solution.py:122
  605.5 14.7 %reshape.276 = bf16[2048,4,512]{2,1,0:T(4,128)(2,1)} reshape(bf16[16,128,2048]{2,1,0:T(8,128)(2,1)} %bitcast.28) | data formatting | bytes 16777216 | tf_op jit(solution)/shard_map/reshape | solution.py:54
  620.2 7.9 fusion.24
  628.2 0.0 reduce-scatter.8.cloned.1.call-update
  628.2 0.2 reduce-scatter.4.cloned.1.call-start
  628.4 8.7 fusion.15
  637.2 6.6 scatter_custom_fusion
  643.8 0.0 reduce-scatter.4.cloned.1.call-update
  643.8 92.8 %reduce-scatter.6.cloned.1.call-done = f32[192,64]{1,0:T(8,128)} async-done(((f32[3072,64]{1,0:T(8,128)}), f32[192,64]{1,0:T(8,128)}) %reduce-scatter.6.cloned.1.call-update) | async-done | bytes 49168 | tf_op jit(solution)/shard_map/reduce_scatter | solution.py:133
  736.5 0.9 convert_bitcast_fusion.1
  737.4 0.7 copy.50
  738.2 58.4 %reduce-scatter.8.cloned.1.call-done = bf16[4,32,128]{2,1,0:T(8,128)(2,1)} async-done(((bf16[4,512,128]{2,1,0:T(8,128)(2,1)}), bf16[4,32,128]{2,1,0:T(8,128)(2,1)}) %reduce-scatter.8.cloned.1.call-update) | async-done | bytes 32784 | tf_op jit(solution)/shard_map/reduce_scatter | solution.py:128
  796.5 1.4 convert_element_type.35
  797.9 225.1 %reduce-scatter.4.cloned.1.call-done = f32[192,512]{1,0:T(8,128)} async-done(((f32[3072,512]{1,0:T(8,128)}), f32[192,512]{1,0:T(8,128)}) %reduce-scatter.4.cloned.1.call-update) | async-done | bytes 393232 | tf_op jit(solution)/shard_map/reduce_scatter | solution.py:132
  1023.0 1.7 convert_bitcast_fusion
  (23 shorter events, 0.1 us)
Async XLA Ops:
  7.2 15.1 %copy-start.4 = (bf16[4,32,128]{2,1,0:T(8,128)(2,1)S(1)}, bf16[4,32,128]{2,1,0:T(8,128)(2,1)}, u32[]{:S(2)}) copy-start(bf16[4,32,128]{2,1,0:T(8,128)(2,1)} %param.13) | copy-start | bytes 98308
  11.2 61.5 %all-to-all-start = ((bf16[128,16,512]{0,2,1:T(8,128)(2,1)}), bf16[128,16,512]{0,2,1:T(8,128)(2,1)S(1)}, u32[]{:S(2)}, u32[]{:S(2)}) async-start(bf16[128,16,512]{0,2,1:T(8,128)(2,1)} %bitcast.102), calls=%async_computation | async-start | bytes 4194304 | tf_op jit(solution)/shard_map/all_to_all | solution.py:123
  78.3 15.3 %copy-start.1 = (bf16[2048,4,128]{0,2,1:T(8,128)(2,1)}, bf16[2048,4,128]{0,2,1:T(8,128)(2,1)S(1)}, u32[]{:S(2)}) copy-start(bf16[2048,4,128]{0,2,1:T(8,128)(2,1)S(1)} %reshape.230) | copy-start | bytes 6291460
  106.2 6.6 copy-start.6
  106.2 305.5 %all-to-all-start.1 = ((bf16[16,128,2048]{2,1,0:T(8,128)(2,1)}), bf16[16,128,2048]{2,1,0:T(8,128)(2,1)}, u32[]{:S(2)}, u32[]{:S(2)}) async-start(bf16[16,128,2048]{2,1,0:T(8,128)(2,1)} %copy.42), calls=%async_computation.1 | async-start | bytes 16777216 | tf_op jit(solution)/shard_map/all_to_all | solution.py:126
  112.0 246.6 %all-gather.4.cloned.1.call-start = ((), (), s32[]{:S(2)}) async-start(), calls=%async_computation.9 | async-start | bytes 3342336 | tf_op jit(solution)/shard_map/all_gather | solution.py:110
  113.1 10.2 copy-start.5
  113.1 242.9 %copy-start.3 = (bf16[1,128,4096]{2,1,0:T(8,128)(2,1)S(1)}, bf16[1,128,4096]{2,1,0:T(8,128)(2,1)}, u32[]{:S(2)}) copy-start(bf16[1,128,4096]{2,1,0:T(8,128)(2,1)} %param.10) | copy-start | bytes 3145732
  113.1 245.3 %copy-start.7 = (s32[1,2]{1,0:T(1,128)S(1)}, s32[1,2]{1,0:T(1,128)}, u32[]{:S(2)}) copy-start(s32[1,2]{1,0:T(1,128)} %param.16) | copy-start | bytes 28
  411.7 193.8 %all-to-all-start.2 = ((bf16[128,16,2048]{2,0,1:T(8,128)(2,1)}), bf16[128,16,2048]{2,0,1:T(8,128)(2,1)}, u32[]{:S(2)}, u32[]{:S(2)}) async-start(bf16[128,16,2048]{2,0,1:T(8,128)(2,1)} %copy.47), calls=%async_computation.4 | async-start | bytes 16777216 | tf_op jit(solution)/shard_map/all_to_all | solution.py:122
  418.5 318.0 %reduce-scatter.6.cloned.1.call-start = ((), (), s32[]{:S(2)}) async-start(), calls=%async_computation.7 | async-start | bytes 1671168 | tf_op jit(solution)/shard_map/reduce_scatter | solution.py:133
  457.7 1.9 copy-start
  464.3 332.2 %reduce-scatter.8.cloned.1.call-start = ((), (), s32[]{:S(2)}) async-start(), calls=%async_computation.8 | async-start | bytes 557056 | tf_op jit(solution)/shard_map/reduce_scatter | solution.py:128
  605.5 14.7 %copy-start.2 = (bf16[2048,4,128]{0,2,1:T(8,128)(2,1)S(1)}, bf16[2048,4,128]{0,2,1:T(8,128)(2,1)}, u32[]{:S(2)}) copy-start(bf16[2048,4,128]{0,2,1:T(8,128)(2,1)} %copy-done.1) | copy-start | bytes 6291460
  628.2 394.8 %reduce-scatter.4.cloned.1.call-start = ((), (), s32[]{:S(2)}) async-start(), calls=%async_computation.6 | async-start | bytes 6684672 | tf_op jit(solution)/shard_map/reduce_scatter | solution.py:132
Sparse Core Ops, SparseCore 0:
  115.4 208.3 all-gather.3
  464.4 272.0 reduce-scatter.5
  739.2 57.2 reduce-scatter.7
  800.5 222.4 reduce-scatter.3
where the time goes:
time: 1040 us; the launch traced here: 1030 us
  waiting for transfers between devices  541 us (52%)
  blocking collectives  250 us (24%)
  local copies, waits for them, and re-layouts  119 us (11%)
  matrix products  62 us (6%)
  starting transfers between devices  24 us (2%)
  other arithmetic  20.5 us (2%)
  between operations  14.8 us (1%)
    all_gather x1, blocking collectives, shards(): lax.all_gather(rope_keys[0], 'ctx', axis=0, tiled=True)  230 us
    reduce_scatter x1, waiting for transfers between devices, shards(): lax.psum_scatter(dense_key, 'ctx', scatter_dimension=0, tiled=True)  225 us
    all_to_all x1, waiting for transfers between devices, shards(): lax.all_to_all(out_latent, 'ctx', split_axis=1, concat_axis=0, tiled=True)  133 us
    reduce_scatter x1, waiting for transfers between devices, shards(): lax.psum_scatter(dense_rope, 'ctx', scatter_dimension=0, tiled=True)  92.8 us
    reduce_scatter x1, waiting for transfers between devices, shards(): lax.psum_scatter(weight_part.astype(jnp.bfloat16), 'dp', scatter_dimensio...  58.4 us
    all_to_all x1, waiting for transfers between devices, shards(): lax.all_to_all(out_grad[0], 'ctx', split_axis=1, concat_axis=0, tiled=True)  31.2 us
    unnamed x22, local copies, waits for them, and re-layouts  26.8 us
    all_to_all x2, local copies, waits for them, and re-layouts, shards(): lax.all_to_all(out_latent, 'ctx', split_axis=1, concat_axis=0, tiled=True)  25.3 us
  transfers between devices with their start and end apart: 7, of which 5 were waited for; matrix products, arithmetic and copies ran while one was open for 14% of the time, Pallas kernels for 0%

commit v1 on v0

v1 whole, which is shorter than its diff:
```python
import functools

import jax
import jax.numpy as jnp
from jax import lax
from jax.experimental import pallas as pl
from jax.experimental.pallas import tpu as pltpu
from jax.sharding import PartitionSpec as P

LAT = 512
ROPE = 64
HD = 128
BLK = 64
SEL = 4
SCALE = (HD + ROPE) ** (-0.5)
ROWS = 224
HALF = ROWS // 2
MESH = pl.DeviceIdType.MESH
BF = jnp.bfloat16
F32 = jnp.float32


def place():
    dp, ctx = lax.axis_index("dp"), lax.axis_index("ctx")
    core, y, x_lo = dp % 2, (dp // 2) % 4, dp // 8
    x_hi, z = ctx // 8, ctx % 8
    return x_hi * 2 + x_lo, y, z, core, x_hi


def device(x, y, z, core):
    return (((x % 2) * 4 + y) * 2 + core, (x // 2) * 8 + z)


class Links:
    def __init__(self, send, recv):
        x, y, z, core, _ = place()
        self.send, self.recv, self.count, self.started = send, recv, 0, []
        self.to = {
            "z": (device(x, y, (z + 1) % 8, core), device(x, y, (z + 7) % 8, core)),
            "y": (device(x, (y + 1) % 4, z, core), device(x, (y + 3) % 4, z, core)),
            "x": (device((x + 1) % 4, y, z, core), device((x + 3) % 4, y, z, core)),
            "far": (device((x + 2) % 4, y, z, core),),
            "core": (device(x, y, z, 1 - core),),
        }

    def barrier(self):
        sem = pltpu.get_barrier_semaphore()
        partners = [d for way in self.to.values() for d in way]
        for d in partners:
            pl.semaphore_signal(sem, inc=1, device_id=d, device_id_type=MESH)
        pl.semaphore_wait(sem, len(partners))

    def push(self, src, dst, way, side=0):
        i = self.count
        self.count += 1
        copy = pltpu.make_async_remote_copy(
            src_ref=src,
            dst_ref=dst,
            send_sem=self.send.at[i],
            recv_sem=self.recv.at[i],
            device_id=self.to[way][side],
            device_id_type=MESH,
        )
        copy.start()
        self.started.append(copy)
        return copy

    def finish(self):
        for copy in self.started:
            copy.wait_send()


def arrive(copies):
    for copy in copies:
        copy.wait_recv()


N_GATHER = 80
N_REDUCE = 80


def gather_kernel(cache_ref, rope_ref, w_ref, kc, g, blk, send, recv, lsem):
    x, y, z, core, xh = place()
    links = Links(send, recv)
    blk[0:192, :] = cache_ref[...]
    packed = [rope_ref[32 * i : 32 * i + 32, :] for i in range(6)]
    blk[192:224, :] = jnp.concatenate(packed + [jnp.zeros((32, 128), BF)], axis=1)
    links.barrier()

    def piece(part, zo):
        return g.at[0, core, y, x, zo] if part == 0 else g.at[1, core, x, y, zo]

    def w_step(s):
        out = []
        for side, sign in ((0, 1), (1, -1)):
            zo = (z - sign * (s - 1) + 8) % 8
            for part in (0, 1):
                src = w_ref.at[part] if s == 1 else piece(part, zo)
                dst = piece(part, zo)
                if s == 4:
                    rows = pl.ds(32 * side, 32)
                    src, dst = src.at[rows], dst.at[rows]
                out.append(links.push(src, dst, "z", side))
        return out

    def c_step(hf, s):
        out = []
        for side, sign in ((0, 1), (1, -1)):
            zo = (z - sign * (s - 1) + 8) % 8
            src = blk if (s == 1 and hf is xh) else kc.at[hf, zo]
            dst = kc.at[hf, zo]
            if s == 4:
                rows = pl.ds(HALF * side, HALF)
                src, dst = src.at[rows], dst.at[rows]
            out.append(links.push(src, dst, "z", side))
        return out

    def ring4(part, way, s, level):
        me = x if way == "x" else y
        out = []
        for side, sign in ((0, 1), (1, -1)):
            o = me if s == 1 else (me - sign + 4) % 4
            if level == 1:
                ref = g.at[part, core, y if part == 0 else x, o]
                if s == 2:
                    ref = ref.at[pl.ds(4 * side, 4)]
            else:
                ref = g.at[part, core, o]
                if s == 2:
                    ref = ref.at[pl.ds(2 * side, 2)]
            out.append(links.push(ref, ref, way, side))
        return out

    other = 1 - xh
    wz = w_step(1)
    c0 = c_step(xh, 1)
    cross = links.push(blk, kc.at[xh, z], "far")
    local = [
        pltpu.make_async_copy(blk, kc.at[xh, z], lsem.at[0]),
        pltpu.make_async_copy(w_ref.at[0], piece(0, z), lsem.at[1]),
        pltpu.make_async_copy(w_ref.at[1], piece(1, z), lsem.at[2]),
    ]
    for copy in local:
        copy.start()
    arrive(wz)
    wz = w_step(2)
    arrive(wz)
    wz = w_step(3)
    arrive(wz)
    wz = w_step(4)
    arrive(c0)
    c0 = c_step(xh, 2)
    arrive(wz)
    for copy in local:
        copy.wait()
    a, b = ring4(0, "x", 1, 1), ring4(1, "y", 1, 1)
    arrive([cross])
    c1 = c_step(other, 1)
    arrive(a)
    a = ring4(0, "x", 2, 1)
    arrive(b)
    b = ring4(1, "y", 2, 1)
    arrive(a)
    a = ring4(0, "y", 1, 2)
    arrive(b)
    b = ring4(1, "x", 1, 2)
    mine = (y, x)
    shared = []

    def share(part, o):
        ref = g.at[part, core, o]
        shared.append(links.push(ref, ref, "core"))

    share(0, y)
    share(1, x)
    arrive(c0)
    c0 = c_step(xh, 3)
    arrive(c1)
    c1 = c_step(other, 2)
    arrive(c0)
    c0 = c_step(xh, 4)
    arrive(c1)
    c1 = c_step(other, 3)
    arrive(a)
    a = ring4(0, "y", 2, 2)
    arrive(b)
    b = ring4(1, "x", 2, 2)
    for part in (0, 1):
        share(part, (mine[part] + 3) % 4)
        share(part, (mine[part] + 1) % 4)
    arrive(c0)
    arrive(c1)
    c1 = c_step(other, 4)
    arrive(a)
    share(0, (y + 2) % 4)
    arrive(b)
    share(1, (x + 2) % 4)
    arrive(c1)
    arrive(shared)
    links.finish()


def gather(cache, rope, weight):
    return pl.pallas_call(
        gather_kernel,
        out_shape=(
            jax.ShapeDtypeStruct((2, 8, ROWS, LAT), BF),
            jax.ShapeDtypeStruct((2, 2, 4, 4, 8, 64, HD), BF),
        ),
        in_specs=[
            pl.BlockSpec(memory_space=pltpu.VMEM),
            pl.BlockSpec(memory_space=pltpu.VMEM),
            pl.BlockSpec(memory_space=pl.ANY),
        ],
        out_specs=(pl.BlockSpec(memory_space=pl.ANY), pl.BlockSpec(memory_space=pl.ANY)),
        scratch_shapes=[
            pltpu.VMEM((ROWS, LAT), BF),
            pltpu.SemaphoreType.DMA((N_GATHER,)),
            pltpu.SemaphoreType.DMA((N_GATHER,)),
            pltpu.SemaphoreType.DMA((3,)),
        ],
        compiler_params=pltpu.CompilerParams(collective_id=0, has_side_effects=True),
        name="gather",
    )(cache, rope, weight)


def reduce_kernel(dc, d, cg_ref, rg_ref, wg_ref, *scratch):
    (acc_c, cin, xin, xout, acc_w, core_in, p1, p2, q1, q2, zin, send, recv, lsem) = scratch
    x, y, z, core, xh = place()
    other = 1 - xh
    links = Links(send, recv)
    links.barrier()
    mine = (y, x)
    local_c = [pltpu.make_async_copy(dc.at[h], acc_c.at[h], lsem.at[i]) for i, h in enumerate((other, xh))]
    for copy in local_c:
        copy.start()
    order = (2, 1, 3, 0)
    local_w, swap = {}, {}
    for k in order:
        for part in (0, 1):
            o = (mine[part] + k) % 4
            swap[part, k] = links.push(d.at[part, 1 - core, o], core_in.at[part, o], "core")
            local_w[part, k] = pltpu.make_async_copy(
                d.at[part, core, o], acc_w.at[part, o], lsem.at[2 + 4 * part + k]
            )
            local_w[part, k].start()

    def add(dst, *srcs):
        total = dst[...].astype(F32)
        for src in srcs:
            total = total + src[...].astype(F32)
        dst[...] = total.astype(BF)

    def c_send(i, hf, s):
        out = []
        for side, sign in ((0, 1), (1, -1)):
            ref = acc_c.at[hf, (z + sign * (5 - s) + 8) % 8]
            dst = cin.at[i, side, s - 1]
            if s == 1:
                rows = pl.ds(HALF * side, HALF)
                ref, dst = ref.at[rows], dst.at[rows]
            out.append(links.push(ref, dst, "z", side))
        return out

    def c_add(i, hf, s):
        for side, sign in ((0, 1), (1, -1)):
            ref = acc_c.at[hf, (z + sign * (4 - s) + 8) % 8]
            src = cin.at[i, side, s - 1]
            if s == 1:
                rows = pl.ds(HALF * side, HALF)
                ref, src = ref.at[rows], src.at[rows]
            add(ref, src)

    def core_add(k):
        for part in (0, 1):
            local_w[part, k].wait()
            swap[part, k].wait_recv()
            o = (mine[part] + k) % 4

            @pl.loop(0, 4)
            def _(i):
                add(acc_w.at[part, o, i], core_in.at[part, o, i])

    def p_send1():
        out = []
        for part, way in ((0, "y"), (1, "x")):
            o = (mine[part] + 2) % 4
            for side in (0, 1):
                rows = pl.ds(2 * side, 2)
                out.append(links.push(acc_w.at[part, o, rows], p1.at[part, side], way, side))
        return out

    def p_add1():
        for part in (0, 1):
            for side, sign in ((0, 1), (1, -1)):
                o = (mine[part] + sign + 4) % 4
                add(acc_w.at[part, o, pl.ds(2 * side, 2)], p1.at[part, side])

    def p_send2():
        out = []
        for part, way in ((0, "y"), (1, "x")):
            for side, sign in ((0, 1), (1, -1)):
                o = (mine[part] + sign + 4) % 4
                out.append(links.push(acc_w.at[part, o], p2.at[part, side], way, side))
        return out

    def p_add2():
        for part in (0, 1):

            @pl.loop(0, 4)
            def _(i):
                add(acc_w.at[part, mine[part], i], p2.at[part, 0, i], p2.at[part, 1, i])

    def q_send1():
        out = []
        for part, way in ((0, "x"), (1, "y")):
            o = (mine[1 - part] + 2) % 4
            for side in (0, 1):
                rows = pl.ds(4 * side, 4)
                out.append(links.push(acc_w.at[part, mine[part], o, rows], q1.at[part, side], way, side))
        return out

    def q_add1():
        for part in (0, 1):
            for side, sign in ((0, 1), (1, -1)):
                o = (mine[1 - part] + sign + 4) % 4
                add(acc_w.at[part, mine[part], o, pl.ds(4 * side, 4)], q1.at[part, side])

    def q_send2():
        out = []
        for part, way in ((0, "x"), (1, "y")):
            for side, sign in ((0, 1), (1, -1)):
                o = (mine[1 - part] + sign + 4) % 4
                out.append(links.push(acc_w.at[part, mine[part], o], q2.at[part, side], way, side))
        return out

    def q_add2():
        for part in (0, 1):
            add(acc_w.at[part, mine[part], mine[1 - part]], q2.at[part, 0], q2.at[part, 1])

    def z_ref(part, zo):
        return acc_w.at[part, mine[part], mine[1 - part], zo]

    def z_send(s):
        out = []
        for part in (0, 1):
            for side, sign in ((0, 1), (1, -1)):
                ref = z_ref(part, (z + sign * (5 - s) + 8) % 8)
                dst = zin.at[part, side, s - 1]
                if s == 1:
                    rows = pl.ds(32 * side, 32)
                    ref, dst = ref.at[rows], dst.at[rows]
                out.append(links.push(ref, dst, "z", side))
        return out

    def z_add(s):
        for part in (0, 1):
            for side, sign in ((0, 1), (1, -1)):
                ref = z_ref(part, (z + sign * (4 - s) + 8) % 8)
                src = zin.at[part, side, s - 1]
                if s == 1:
                    rows = pl.ds(32 * side, 32)
                    ref, src = ref.at[rows], src.at[rows]
                add(ref, src)

    for copy in local_c:
        copy.wait()
    c1 = c_send(0, other, 1)
    c0 = c_send(1, xh, 1)
    core_add(2)
    w = p_send1()
    core_add(1)
    core_add(3)
    arrive(c1)
    c_add(0, other, 1)
    c1 = c_send(0, other, 2)
    arrive(c0)
    c_add(1, xh, 1)
    c0 = c_send(1, xh, 2)
    arrive(w)
    p_add1()
    w = p_send2()
    core_add(0)
    arrive(c1)
    c_add(0, other, 2)
    c1 = c_send(0, other, 3)
    arrive(c0)
    c_add(1, xh, 2)
    c0 = c_send(1, xh, 3)
    arrive(w)
    p_add2()
    w = q_send1()
    arrive(c1)
    c_add(0, other, 3)
    c1 = c_send(0, other, 4)
    arrive(w)
    q_add1()
    w = q_send2()
    arrive(c0)
    c_add(1, xh, 3)
    arrive(w)
    q_add2()
    w = z_send(1)
    arrive(c1)
    total = acc_c[other, z].astype(F32) + cin[0, 0, 3].astype(F32) + cin[0, 1, 3].astype(F32)
    xout[...] = total.astype(BF)
    cross = links.push(xout, xin, "far")
    c0 = c_send(1, xh, 4)
    for s in (1, 2, 3):
        arrive(w)
        z_add(s)
        w = z_send(s + 1)
    arrive(w)
    for part in (0, 1):
        total = z_ref(part, z)[...].astype(F32)
        for side in (0, 1):
            total = total + zin[part, side, 3].astype(F32)
        wg_ref[part] = total
    arrive([cross])
    arrive(c0)
    total = acc_c[xh, z].astype(F32) + cin[1, 0, 3].astype(F32) + cin[1, 1, 3].astype(F32)
    total = (total + xin[...].astype(F32)).astype(BF)
    cg_ref[...] = total[0:192]
    for i in range(6):
        rg_ref[32 * i : 32 * i + 32, :] = total[192:224, 64 * i : 64 * i + 64]
    links.finish()


def reduce(dc, d):
    half = (2, 4, 4, 8, 64, HD)
    return pl.pallas_call(
        reduce_kernel,
        out_shape=(
            jax.ShapeDtypeStruct((192, LAT), BF),
            jax.ShapeDtypeStruct((192, ROPE), BF),
            jax.ShapeDtypeStruct((2, 64, HD), F32),
        ),
        in_specs=[pl.BlockSpec(memory_space=pl.ANY)] * 2,
        out_specs=(pl.BlockSpec(memory_space=pltpu.VMEM),) * 3,
        scratch_shapes=[
            pltpu.VMEM((2, 8, ROWS, LAT), BF),
            pltpu.VMEM((2, 2, 4, ROWS, LAT), BF),
            pltpu.VMEM((ROWS, LAT), BF),
            pltpu.VMEM((ROWS, LAT), BF),
            pltpu.VMEM(half, BF),
            pltpu.VMEM(half, BF),
            pltpu.VMEM((2, 2, 2, 8, 64, HD), BF),
            pltpu.VMEM((2, 2, 4, 8, 64, HD), BF),
            pltpu.VMEM((2, 2, 4, 64, HD), BF),
            pltpu.VMEM((2, 2, 8, 64, HD), BF),
            pltpu.VMEM((2, 2, 4, 64, HD), BF),
            pltpu.SemaphoreType.DMA((N_REDUCE,)),
            pltpu.SemaphoreType.DMA((N_REDUCE,)),
            pltpu.SemaphoreType.DMA((10,)),
        ],
        compiler_params=pltpu.CompilerParams(
            collective_id=1, has_side_effects=True, vmem_limit_bytes=40 * 2**20
        ),
        name="reduce",
    )(dc, d)


NT = (((1,), (1,)), ((), ()))
NN = (((1,), (0,)), ((), ()))


def dot(a, b, dims):
    return lax.dot_general(a, b, dims, preferred_element_type=F32)


def attend_kernel(ids, counts, q, qr, og, kc, w, dc, d, k, kt, rpk, r, bias, dk, dr, dense, sem):
    step = pl.program_id(0)
    xh = step % 2

    @pl.when(step == 0)
    def _():
        copies = []
        for b in range(2):
            for j in range(SEL):
                block = ids[b, j]
                owner, part = block // 3, block % 3
                rows = pl.ds(pl.multiple_of(part * 64, 64), 64)
                lanes = pl.ds(pl.multiple_of(part * 128, 128), 128)
                n = 2 * (b * SEL + j)
                copies.append(
                    pltpu.make_async_copy(kc.at[owner, rows], k.at[b, pl.ds(64 * j, 64)], sem.at[n])
                )
                copies.append(
                    pltpu.make_async_copy(kc.at[owner, pl.ds(192, 32), lanes], rpk.at[b, j], sem.at[n + 1])
                )
        for copy in copies:
            copy.start()
        row = lax.broadcasted_iota(jnp.int32, (256, 256), 0)
        col = lax.broadcasted_iota(jnp.int32, (256, 256), 1)
        for b in range(2):
            slot = row // 64
            causal = jnp.where(row % 64 <= col % 64, 0.0, -1e30).astype(F32)
            listed = jnp.where(slot < counts[b], 0.0, -1e30).astype(F32)
            bias[b] = jnp.where(slot == 0, causal, listed)
        dk[...] = jnp.zeros_like(dk)
        dr[...] = jnp.zeros_like(dr)
        for copy in copies:
            copy.wait()
        for b in range(2):
            kt[b] = k[b].T
            for j in range(SEL):
                r[b, 64 * j : 64 * j + 32, :] = rpk[b, j, :, 0:64]
                r[b, 64 * j + 32 : 64 * j + 64, :] = rpk[b, j, :, 64:128]

    spots = [(x_lo, y, core) for x_lo in range(2) for y in range(4) for core in range(2)]

    def at(part, x_lo, y, core):
        xx = 2 * xh + x_lo
        return (0, core, y, xx, 0) if part == 0 else (1, core, xx, y, 0)

    columns = []
    for head in range(4):
        part, low = head // 2, 32 * (head % 2)
        columns.append(
            jnp.concatenate([w[at(part, *spot) + (slice(low, low + 32),)] for spot in spots], axis=0)
        )
    weight = jnp.concatenate(columns, axis=1)
    dw = None
    for b in range(2):
        rows = slice(64 * b, 64 * b + 64)
        qs = jnp.concatenate([q[rows, LAT * h : LAT * h + LAT] for h in range(4)], axis=0)
        qrs = jnp.concatenate([qr[rows, ROPE * h : ROPE * h + ROPE] for h in range(4)], axis=0)
        zero = jnp.zeros((64, HD), BF)
        gd = jnp.concatenate(
            [
                jnp.concatenate(
                    [og[rows, HD * h : HD * h + HD] if i == h else zero for i in range(4)], axis=1
                )
                for h in range(4)
            ],
            axis=0,
        )
        keys = k[b]
        s = (dot(keys, qs, NT) + dot(r[b], qrs, NT)) * SCALE + bias[b]
        e = jnp.exp(s - jnp.max(s, axis=0, keepdims=True))
        prob = e * (1.0 / jnp.sum(e, axis=0, keepdims=True))
        half = prob.astype(BF)
        out_t = dot(kt[b], half, NN).astype(BF)
        part_w = dot(out_t, gd, NN)
        dw = part_w if dw is None else dw + part_w
        back = dot(gd, weight, NT).astype(BF)
        dp = dot(keys, back, NT)
        delta = jnp.sum(prob * dp, axis=0, keepdims=True)
        ds = (prob * (dp - delta)).astype(BF)
        dk[b] += dot(half, back, NN) + SCALE * dot(ds, qs, NN)
        dr[b] += dot(ds, qrs, NN)
    dw = dw.astype(BF)
    for head in range(4):
        part, low = head // 2, 32 * (head % 2)
        for i, spot in enumerate(spots):
            d[at(part, *spot) + (slice(low, low + 32),)] = dw[32 * i : 32 * i + 32, HD * head : HD * head + HD]

    @pl.when(step == pl.num_programs(0) - 1)
    def _():
        dense[...] = jnp.zeros_like(dense)
        for b in range(2):
            for j in range(SEL):
                block = ids[b, j]
                owner, part = block // 3, block % 3
                rows = pl.ds(pl.multiple_of(part * 64, 64), 64)
                dense[owner, rows, :] += dk[b, 64 * j : 64 * j + 64, :]
                lanes = pl.ds(pl.multiple_of(part * 128, 128), 128)
                low = dr[b, 64 * j : 64 * j + 32, :]
                high = dr[b, 64 * j + 32 : 64 * j + 64, :]
                dense[owner, 192:224, lanes] += SCALE * jnp.concatenate([low, high], axis=1)
        dc[...] = dense[...].astype(BF)


def attend(ids, counts, q, qr, og, kc, g):
    def group(i):
        return (i % 2) * 8 + i // 2

    gshape = (2, 2, 4, 4, 8, 64, HD)
    gblock = (2, 2, 4, 4, 1, 64, HD)
    return pl.pallas_call(
        attend_kernel,
        grid_spec=pltpu.PrefetchScalarGridSpec(
            num_scalar_prefetch=2,
            grid=(16,),
            in_specs=[
                pl.BlockSpec((128, 4 * LAT), lambda i, *_: (0, group(i))),
                pl.BlockSpec((128, 4 * ROPE), lambda i, *_: (0, group(i))),
                pl.BlockSpec((128, 4 * HD), lambda i, *_: (0, group(i))),
                pl.BlockSpec(memory_space=pl.ANY),
                pl.BlockSpec(gblock, lambda i, *_: (0, 0, 0, 0, i // 2, 0, 0)),
            ],
            out_specs=(
                pl.BlockSpec((16, ROWS, LAT), lambda i, *_: (0, 0, 0)),
                pl.BlockSpec(gblock, lambda i, *_: (0, 0, 0, 0, i // 2, 0, 0)),
            ),
            scratch_shapes=[
                pltpu.VMEM((2, 256, LAT), BF),
                pltpu.VMEM((2, LAT, 256), BF),
                pltpu.VMEM((2, SEL, 32, 128), BF),
                pltpu.VMEM((2, 256, ROPE), BF),
                pltpu.VMEM((2, 256, 256), F32),
                pltpu.VMEM((2, 256, LAT), F32),
                pltpu.VMEM((2, 256, ROPE), F32),
                pltpu.VMEM((16, ROWS, LAT), F32),
                pltpu.SemaphoreType.DMA((16,)),
            ],
        ),
        out_shape=(
            jax.ShapeDtypeStruct((16, ROWS, LAT), BF),
            jax.ShapeDtypeStruct(gshape, BF),
        ),
        compiler_params=pltpu.CompilerParams(vmem_limit_bytes=48 * 2**20),
        name="attend",
    )(ids, counts, q, qr, og, kc, g)


def shards(
    q_latent,
    q_rope,
    latent_cache,
    rope_keys,
    up_weight,
    out_grad,
    block_ids,
    block_counts,
    slab_offset,
):
    kc, g = gather(latent_cache[0], rope_keys[0], up_weight.reshape(2, 64, HD))
    dc, d = attend(
        block_ids[0],
        block_counts[0],
        q_latent[0],
        q_rope[0],
        out_grad[0],
        kc.reshape(16, ROWS, LAT),
        g,
    )
    cg, rg, wg = reduce(dc.reshape(2, 8, ROWS, LAT), d)
    return cg[None], rg[None], wg.reshape(4, 32, HD)


def solution(mesh):
    placed = (
        P("dp", "ctx", None),
        P("dp", "ctx", None),
        P("dp", "ctx", None),
        P("dp", "ctx", None),
        P("ctx", "dp", None),
        P("dp", "ctx", None),
        P("dp", "ctx", None),
        P("dp", "ctx"),
        P("dp"),
    )
    return jax.shard_map(
        shards,
        mesh=mesh,
        in_specs=placed,
        out_specs=(P("dp", "ctx", None), P("dp", "ctx", None), P("ctx", "dp", None)),
        check_vma=False,
    )
```

time: 1040 us -> 183 us (0.18)
  waiting for transfers between devices: 541 us -> 0 us
  blocking collectives: 250 us -> 0 us
  Pallas kernels: 0 us -> 169 us
  local copies, waits for them, and re-layouts: 119 us -> 13.1 us
  matrix products: 62 us -> 0 us
  starting transfers between devices: 24 us -> 0 us
  other arithmetic: 20.5 us -> 0 us
  between operations: 14.8 us -> 0.68 us
    reduce_scatter x3 -> x0, waiting for transfers between devices: 376 us -> none  [the longest x1 225 us: shards(): lax.psum_scatter(dense_key, 'ctx', scatter_dimension=0, tiled=True)]
    all_gather x2 -> x0, blocking collectives: 250 us -> none  [the longest x1 230 us: shards(): lax.all_gather(rope_keys[0], 'ctx', axis=0, tiled=True)]
    pallas_call x0 -> x3, Pallas kernels: none -> 169 us  [the longest x1 58.6 us: gather(): pl.pallas_call(gather_kernel, out_shape=(jax.ShapeDtypeStruct((2, 8, ROWS...]
    all_to_all x3 -> x0, waiting for transfers between devices: 164 us -> none  [the longest x1 133 us: shards(): lax.all_to_all(out_latent, 'ctx', split_axis=1, concat_axis=0, tiled=True)]
    dot_general x8 -> x0, matrix products: 54.5 us -> none  [the longest x1 9.04 us: attend(): jnp.einsum('bthl,bkl->bthk', q_tiles, key_tiles, preferred_element_type=j...]
    all_to_all x5 -> x0, local copies, waits for them, and re-layouts: 51.7 us -> none  [the longest x2 25.3 us: shards(): lax.all_to_all(out_latent, 'ctx', split_axis=1, concat_axis=0, tiled=True)]
    reshape x4 -> x0, local copies, waits for them, and re-layouts: 32 us -> none  [the longest x1 14.7 us: project(): latent_rows = out_latent.reshape(-1, head_count, LAT)]
    all_to_all x3 -> x0, starting transfers between devices: 23.7 us -> none  [the longest x1 11 us: shards(): lax.all_to_all(out_grad[0], 'ctx', split_axis=1, concat_axis=0, tiled=True)]
  transfers between devices with their start and end apart: 7 -> 0, of which waited for: 5 -> 0; matrix products, arithmetic and copies ran while one was open for 14% -> 0% of each run, Pallas kernels for 0% -> 0%
where the time goes in v1:
time: 183 us; the launch traced here: 182 us
  Pallas kernels  169 us (92%)
  local copies, waits for them, and re-layouts  13.1 us (7%)
    pallas_call x1, Pallas kernels, gather(): pl.pallas_call(gather_kernel, out_shape=(jax.ShapeDtypeStruct((2, 8, ROWS...  58.6 us
    pallas_call x1, Pallas kernels, attend(): pl.pallas_call(attend_kernel, grid_spec=pltpu.PrefetchScalarGridSpec(num_...  58.1 us
    pallas_call x1, Pallas kernels, reduce(): pl.pallas_call(reduce_kernel, out_shape=(jax.ShapeDtypeStruct((192, LAT),...  51.9 us
    unnamed x16, local copies, waits for them, and re-layouts  13.1 us

profile of v1, /device:TPU:8, one launch (start us, length us, event | category | flops | bytes accessed | tf_op | source)
XLA Modules:
  0.0 182.3 jit_solution(11564102777050166742)
XLA Ops:
  0.6 1.5 copy.11
  2.1 58.6 %gather.1 = (bf16[2,8,224,512]{3,2,1,0:T(8,128)(2,1)}, bf16[2,2,4,4,8,64,128]{6,5,4,3,2,1,0:T(8,128)(2,1)}) custom-call(bf16[192,512]{1,0:T(8,128)(2,1)} %bitcast.23, bf16[192,64]{1,0:T(8,128)(2,1)} %bitcast.24, bf16[2,64,128]{2,1,0:T(8,128)(2,1)} %bitcast.25), custom_call_target="tpu_custom_call" | custom-call | tf_op jit(solution)/shard_map/gather/pallas_call | solution.py:204
  60.7 0.0 copy-start.2
  60.7 1.6 copy-done.2
  62.3 0.0 copy-start.3
  62.3 1.2 copy-done.3
  63.5 0.0 copy-start.4
  63.5 0.7 copy-done.4
  64.2 0.0 copy-start.5
  64.2 0.7 copy-done.5
  64.8 58.1 %attend.1 = (bf16[16,224,512]{2,1,0:T(8,128)(2,1)}, bf16[2,2,4,4,8,64,128]{6,5,4,3,2,1,0:T(8,128)(2,1)}) custom-call(s32[2,4]{1,0:T(2,128)S(1)} %bitcast.19, s32[2]{0:T(128)S(1)} %bitcast.20, bf16[128,32768]{1,0:T(8,128)(2,1)} %bitcast.21, bf16[128,4096]{1,0:T(8,128)(2,1)S(1)} %bitcast.15, bf16[128,8192]{1,0:T(8,128)(2,1)S(1)} %bitcast.14, ...), custom_call_target="tpu_custom_call" | custom-call | tf_op jit(solution)/shard_map/attend/pallas_call | solution.py:580
  123.0 0.0 copy-start
  123.0 3.4 %copy-done = bf16[2,2,4,4,8,64,128]{6,5,4,3,2,1,0:T(8,128)(2,1)S(1)} copy-done((bf16[2,2,4,4,8,64,128]{6,5,4,3,2,1,0:T(8,128)(2,1)S(1)}, bf16[2,2,4,4,8,64,128]{6,5,4,3,2,1,0:T(8,128)(2,1)}, u32[]{:S(2)}) %copy-start) | copy-done | bytes 8388632
  126.4 0.0 copy-start.1
  126.4 2.0 %copy-done.1 = bf16[16,224,512]{2,1,0:T(8,128)(2,1)S(1)} copy-done((bf16[16,224,512]{2,1,0:T(8,128)(2,1)S(1)}, bf16[16,224,512]{2,1,0:T(8,128)(2,1)}, u32[]{:S(2)}) %copy-start.1) | copy-done | bytes 3670040
  128.4 51.9 %reduce.1 = (bf16[192,512]{1,0:T(8,128)(2,1)S(1)}, bf16[192,64]{1,0:T(8,128)(2,1)S(1)}, f32[2,64,128]{2,1,0:T(8,128)S(1)}) custom-call(bf16[2,8,224,512]{3,2,1,0:T(8,128)(2,1)S(1)} %bitcast.13, bf16[2,2,4,4,8,64,128]{6,5,4,3,2,1,0:T(8,128)(2,1)S(1)} %copy-done), custom_call_target="tpu_custom_call" | custom-call | tf_op jit(solution)/shard_map/reduce/pallas_call | solution.py:431
  180.3 0.7 copy.12
  181.0 0.7 copy.15
  181.7 0.6 copy.16
Async XLA Ops:
  60.7 1.6 copy-start.2
  62.3 1.2 copy-start.3
  63.5 0.7 copy-start.4
  64.2 0.7 copy-start.5
  123.0 3.4 %copy-start = (bf16[2,2,4,4,8,64,128]{6,5,4,3,2,1,0:T(8,128)(2,1)S(1)}, bf16[2,2,4,4,8,64,128]{6,5,4,3,2,1,0:T(8,128)(2,1)}, u32[]{:S(2)}) copy-start(bf16[2,2,4,4,8,64,128]{6,5,4,3,2,1,0:T(8,128)(2,1)} %get-tuple-element.13.d) | copy-start | bytes 25165828
  126.4 2.0 %copy-start.1 = (bf16[16,224,512]{2,1,0:T(8,128)(2,1)S(1)}, bf16[16,224,512]{2,1,0:T(8,128)(2,1)}, u32[]{:S(2)}) copy-start(bf16[16,224,512]{2,1,0:T(8,128)(2,1)} %get-tuple-element.12) | copy-start | bytes 11010052

commit v2 on v0

v2 whole, which is shorter than its diff:
```python
import functools

import jax
import jax.numpy as jnp
from jax import lax
from jax.experimental import pallas as pl
from jax.experimental.pallas import tpu as pltpu
from jax.sharding import PartitionSpec as P

LAT = 512
ROPE = 64
HD = 128
BLK = 64
SEL = 4
SCALE = (HD + ROPE) ** (-0.5)
TILES = 14
HALF = TILES // 2
MESH = pl.DeviceIdType.MESH
BF = jnp.bfloat16
F32 = jnp.float32


def place():
    dp, ctx = lax.axis_index("dp"), lax.axis_index("ctx")
    core, y, x_lo = dp % 2, (dp // 2) % 4, dp // 8
    x_hi, z = ctx // 8, ctx % 8
    return x_hi * 2 + x_lo, y, z, core, x_hi


def device(x, y, z, core):
    return (((x % 2) * 4 + y) * 2 + core, (x // 2) * 8 + z)


class Links:
    def __init__(self, send, recv):
        x, y, z, core, _ = place()
        self.send, self.recv, self.count, self.started = send, recv, 0, []
        self.to = {
            "z": (device(x, y, (z + 1) % 8, core), device(x, y, (z + 7) % 8, core)),
            "y": (device(x, (y + 1) % 4, z, core), device(x, (y + 3) % 4, z, core)),
            "x": (device((x + 1) % 4, y, z, core), device((x + 3) % 4, y, z, core)),
            "far": (device((x + 2) % 4, y, z, core),),
            "core": (device(x, y, z, 1 - core),),
        }
        for n in range(1, 8):
            self.to["z", n] = (device(x, y, (z + n) % 8, core),)

    def barrier(self):
        sem = pltpu.get_barrier_semaphore()
        partners = [d for way, group in self.to.items() if way != "z" for d in group]
        for d in partners:
            pl.semaphore_signal(sem, inc=1, device_id=d, device_id_type=MESH)
        pl.semaphore_wait(sem, len(partners))

    def push(self, src, dst, way, side=0, start=True):
        i = self.count
        self.count += 1
        copy = pltpu.make_async_remote_copy(
            src_ref=src,
            dst_ref=dst,
            send_sem=self.send.at[i],
            recv_sem=self.recv.at[i],
            device_id=self.to[way][side],
            device_id_type=MESH,
        )
        if start:
            copy.start()
        self.started.append(copy)
        return copy

    def finish(self):
        for copy in self.started:
            copy.wait_send()


def arrive(copies):
    for copy in copies:
        copy.wait_recv()


NT = (((1,), (1,)), ((), ()))
NN = (((1,), (0,)), ((), ()))


def dot(a, b, dims):
    return lax.dot_general(a, b, dims, preferred_element_type=F32)


def lanes_of(c, width):
    return pl.ds(pl.multiple_of(c * width, width), width)


SPOTS = [(x_lo, y, core) for x_lo in range(2) for y in range(4) for core in range(2)]


def weight_at(part, xh, x_lo, y, core, z):
    return (core, y, 2 * xh + x_lo, z, slice(64 * part, 64 * part + 64))


def grad_at(part, xh, x_lo, y, core, z):
    xx = 2 * xh + x_lo
    return (0, core, y, xx, z) if part == 0 else (1, core, xx, y, z)


def grads_of_pair(og, i, xh, part):
    low = og[:, lanes_of((xh * 8 + i) * 2 + part, 2 * HD)]
    zero = jnp.zeros((64, HD), BF)
    rows = []
    for b in range(2):
        first, second = low[64 * b : 64 * b + 64, :HD], low[64 * b : 64 * b + 64, HD:]
        rows.append(jnp.concatenate([first, zero], axis=1))
        rows.append(jnp.concatenate([zero, second], axis=1))
    return jnp.concatenate(rows, axis=0)


def queries(q, i, b):
    parts = []
    for xh in range(2):
        block = q[64 * b : 64 * b + 64, lanes_of(xh * 8 + i, 4 * LAT)]
        parts += [block[:, LAT * j : LAT * j + LAT] for j in range(4)]
    return jnp.concatenate(parts, axis=0)


def rotary(qr, i, b):
    low = lax.broadcasted_iota(jnp.int32, (64, 128), 1) < 64
    parts = []
    for xh in range(2):
        block = qr[64 * b : 64 * b + 64, lanes_of(xh * 8 + i, 4 * ROPE)].astype(F32)
        for j in range(4):
            slab = block[:, 128 * (j // 2) : 128 * (j // 2) + 128]
            slab = jnp.where(low, slab, 0.0) if j % 2 == 0 else jnp.where(low, 0.0, slab)
            parts.append(slab.astype(BF))
    return jnp.concatenate(parts, axis=0)


def forward(i, q, qr, og, k, kt, bias, ph, d):
    outs = []
    for b in range(2):
        qs = jnp.concatenate([queries(q, i, b), rotary(qr, i, b)], axis=1)
        s = dot(k[b], qs, NT) * SCALE + jnp.concatenate([bias[b]] * 4, axis=1)
        e = jnp.exp(s - jnp.max(s, axis=0, keepdims=True))
        half = (e * (1.0 / jnp.sum(e, axis=0, keepdims=True))).astype(BF)
        ph[i, b] = half
        outs.append(dot(kt[b], half, NN).astype(BF))
    for pair in range(4):
        xh, part = pair // 2, pair % 2
        both = jnp.concatenate([out[:, 128 * pair : 128 * pair + 128] for out in outs], axis=1)
        dw = dot(both, grads_of_pair(og, i, xh, part), NN).astype(BF)
        for n, spot in enumerate(SPOTS):
            rows = dw[32 * n : 32 * n + 32]
            d[grad_at(part, xh, *spot, i)] = jnp.concatenate([rows[:, :HD], rows[:, HD:]], axis=0)


def backward(i, q, qr, og, k, w, ph, dk, dr):
    backs = []
    for pair in range(4):
        xh, part = pair // 2, pair % 2
        pieces = [w[weight_at(part, xh, *spot, i)] for spot in SPOTS]
        weight = jnp.concatenate(
            [jnp.concatenate([p[:32], p[32:]], axis=1) for p in pieces], axis=0
        )
        backs.append(dot(grads_of_pair(og, i, xh, part), weight, NT).astype(BF))
    for b in range(2):
        back = jnp.concatenate([back[128 * b : 128 * b + 128] for back in backs], axis=0)
        dp = dot(k[b, :, :LAT], back, NT)
        half = ph[i, b]
        prob = half.astype(F32)
        weighted = prob * dp
        delta = jnp.sum(weighted, axis=0, keepdims=True)
        ds = ((weighted - prob * delta) * SCALE).astype(BF)
        dk[b] += dot(
            jnp.concatenate([half, ds], axis=1), jnp.concatenate([back, queries(q, i, b)], axis=0), NN
        )
        dr[b] += dot(ds, rotary(qr, i, b), NN)


def core_kernel(
    ids, counts, cache, rope, w_in, q_hbm, qr_hbm, og_hbm, cg, rg, wg,
    kc, g, d, core_in, q, qr, og, rope_v, k, kt, bias, ph, dk, dr, drp, cin, p1, p2, q1, q2, zin,
    send, recv, lsem,
):
    x, y, z, core, xh = place()
    links = Links(send, recv)
    mine = (y, x)

    def own(n):
        return xh * 8 + (z + n + 8) % 8

    def oth(n):
        return (1 - xh) * 8 + (z + n + 8) % 8

    def upper(side):
        return pl.ds(HALF * side, HALF)

    first = [
        pltpu.make_async_copy(cache, kc.at[own(0), pl.ds(0, 12)], lsem.at[0]),
        pltpu.make_async_copy(rope, rope_v, lsem.at[1]),
        pltpu.make_async_copy(w_in, g.at[core, y, x, z], lsem.at[2]),
    ]
    loads = [
        pltpu.make_async_copy(qr_hbm, qr, lsem.at[4]),
        pltpu.make_async_copy(og_hbm, og, lsem.at[5]),
        pltpu.make_async_copy(q_hbm, q, lsem.at[6]),
    ]
    for copy in first + loads:
        copy.start()
    links.barrier()
    for copy in first:
        copy.wait()
    flipped = jnp.concatenate([rope_v[...].astype(F32), jnp.zeros((ROPE, 64), F32)], axis=1)
    flipped = jnp.concatenate([flipped, jnp.zeros((128 - ROPE, 256), F32)], axis=0).T
    packed = [flipped[32 * i : 32 * i + 32, :ROPE].astype(BF) for i in range(6)]
    packed = jnp.concatenate(packed + [jnp.zeros((32, 128), BF)], axis=1)
    kc[own(0), 12] = packed[:16]
    kc[own(0), 13] = packed[16:]

    def ring_x(s):
        out = []
        for side, sign in ((0, 1), (1, -1)):
            if s == 1:
                ref = g.at[core, y, x]
            else:
                ref = g.at[core, y, (x - sign + 4) % 4, pl.ds(4 * side, 4)]
            out.append(links.push(ref, ref, "x", side))
        return out

    def ring_y1(n):
        ref = g.at[core, y, (x + n + 4) % 4]
        return [links.push(ref, ref, "y", side) for side in (0, 1)]

    def ring_y2(n, start=True):
        out = []
        for side, sign in ((0, 1), (1, -1)):
            ref = g.at[core, (y - sign + 4) % 4, (x + n + 4) % 4, pl.ds(4 * side, 4)]
            out.append(links.push(ref, ref, "y", side, start))
        return out

    shared = []

    def share(n, start=True):
        ref = g.at[core, (y + n) % 4]
        shared.append(links.push(ref, ref, "core", 0, start))
        return shared[-1]

    def ring8(s):
        out = []
        for side, sign in ((0, 1), (1, -1)):
            ref = kc.at[own(-sign * (s - 1))]
            if s == 4:
                ref = ref.at[upper(side)]
            out.append(links.push(ref, ref, "z", side))
        return out

    def push_block(o, way, side=0, rows=None):
        ref = kc.at[o]
        if rows is not None:
            ref = ref.at[rows]
        return links.push(ref, ref, way, side)

    weights = g.at[core, y, x, z]
    c = ring8(1)
    cross0 = push_block(own(0), "far")
    wz = [links.push(weights, weights, ("z", n)) for n in (4, 3, 5, 2, 6, 1, 7)]
    arrive(c)
    c = ring8(2)
    cross1 = [push_block(own(1), "far", 0, upper(0)), push_block(own(-1), "far", 0, upper(1))]
    arrive(wz)
    ya = ring_y1(0)
    wx = ring_x(1)
    arrive([cross0])
    near = [push_block(oth(0), "z", 0, upper(0)), push_block(oth(0), "z", 1, upper(1))]
    arrive(c)
    c = ring8(3)
    cross2 = [push_block(own(2), "far"), push_block(own(-2), "far")]
    arrive(ya)
    ya2 = ring_y2(0)
    arrive(wx)
    wx = ring_x(2)
    yb = ring_y1(1) + ring_y1(-1)
    arrive(c)
    c = ring8(4)
    arrive(c)
    cross4 = push_block(own(4), "far")
    arrive(wx)
    yc = ring_y1(2)
    share(0)
    arrive(cross2)
    third = [push_block(oth(-2), "z", 0), push_block(oth(2), "z", 1)]
    arrive(yb)
    yb2 = ring_y2(1) + ring_y2(-1)
    row = lax.broadcasted_iota(jnp.int32, (256, 128), 0)
    col = lax.broadcasted_iota(jnp.int32, (256, 128), 1)
    for n in range(2):
        slot = row // 64
        causal = jnp.where(row % 64 <= col % 64, 0.0, -1e30).astype(F32)
        listed = jnp.where(slot < counts[n], 0.0, -1e30).astype(F32)
        bias[n] = jnp.where(slot == 0, causal, listed)
    dk[...] = jnp.zeros_like(dk)
    dr[...] = jnp.zeros_like(dr)
    for copy in loads:
        copy.wait()
    arrive(cross1)
    arrive(near)
    arrive([cross4])
    arrive(third)

    for n in range(2):
        for j in range(SEL):
            owner, part = lax.div(ids[n, j], 3), lax.rem(ids[n, j], 3)
            for r in range(4):
                k[n, 64 * j + 16 * r : 64 * j + 16 * r + 16, :LAT] = kc[owner, 4 * part + r]
            for r in range(2):
                packs = kc[owner, 12 + r].astype(F32)
                pack = packs[:, 256:384]
                pack = jnp.where(part == 0, packs[:, 0:128], pack)
                pack = jnp.where(part == 1, packs[:, 128:256], pack)
                low, high = pack[:, :64].astype(BF), pack[:, 64:].astype(BF)
                row = 64 * j + 16 * r
                k[n, row : row + 16, LAT:] = jnp.concatenate([low, low], axis=1)
                k[n, row + 32 : row + 48, LAT:] = jnp.concatenate([high, high], axis=1)
        kt[n] = k[n, :, :LAT].T

    first_swap = links.count
    links.count += 8

    def swap(i):
        return pltpu.make_async_remote_copy(
            src_ref=d.at[:, 1 - core, :, :, i],
            dst_ref=core_in.at[:, :, :, i],
            send_sem=send.at[first_swap + i],
            recv_sem=recv.at[first_swap + i],
            device_id=links.to["core"][0],
            device_id_type=MESH,
        )

    def add(dst, *srcs):
        total = dst[...].astype(F32)
        for src in srcs:
            total = total + src[...].astype(F32)
        dst[...] = total.astype(BF)

    def swap_add(i):
        swap(i).wait_recv()
        for part in (0, 1):
            for n in range(4):
                add(d.at[part, core, n, :, i], core_in.at[part, n, :, i])

    def p_send1(h, start=True):
        out = []
        for part, way in ((0, "y"), (1, "x")):
            for side in (0, 1):
                ref = d.at[part, core, (mine[part] + 2) % 4, pl.ds(2 * side, 2), pl.ds(4 * h, 4)]
                out.append(links.push(ref, p1.at[h, part, side], way, side, start))
        return out

    def p_add1(h):
        for part in (0, 1):
            for side, sign in ((0, 1), (1, -1)):
                o = (mine[part] + sign + 4) % 4
                for n in range(2):
                    add(d.at[part, core, o, 2 * side + n, pl.ds(4 * h, 4)], p1.at[h, part, side, n])

    def p_send2(h, start=True):
        out = []
        for part, way in ((0, "y"), (1, "x")):
            for side, sign in ((0, 1), (1, -1)):
                ref = d.at[part, core, (mine[part] + sign + 4) % 4, :, pl.ds(4 * h, 4)]
                out.append(links.push(ref, p2.at[h, part, side], way, side, start))
        return out

    def p_add2(h):
        for part in (0, 1):
            for n in range(4):
                ref = d.at[part, core, mine[part], n, pl.ds(4 * h, 4)]
                add(ref, p2.at[h, part, 0, n], p2.at[h, part, 1, n])

    def q_send1():
        out = []
        for part, way in ((0, "x"), (1, "y")):
            o = (mine[1 - part] + 2) % 4
            for side in (0, 1):
                rows = pl.ds(4 * side, 4)
                out.append(links.push(d.at[part, core, mine[part], o, rows], q1.at[part, side], way, side))
        return out

    def q_add1():
        for part in (0, 1):
            for side, sign in ((0, 1), (1, -1)):
                o = (mine[1 - part] + sign + 4) % 4
                add(d.at[part, core, mine[part], o, pl.ds(4 * side, 4)], q1.at[part, side])

    def q_send2():
        out = []
        for part, way in ((0, "x"), (1, "y")):
            for side, sign in ((0, 1), (1, -1)):
                o = (mine[1 - part] + sign + 4) % 4
                out.append(links.push(d.at[part, core, mine[part], o], q2.at[part, side], way, side))
        return out

    def q_add2():
        for part in (0, 1):
            add(d.at[part, core, mine[part], mine[1 - part]], q2.at[part, 0], q2.at[part, 1])

    def total_of(part):
        total = d[part, core, mine[part], mine[1 - part], z].astype(F32)
        for n in range(7):
            total = total + zin[part, n].astype(F32)
        return total

    yc2 = ring_y2(2, False)
    late = [share(1, False), share(3, False), share(2, False)]
    pa1 = p_send1(0, False)

    @pl.loop(0, 8)
    def _(i):
        forward(i, q, qr, og, k, kt, bias, ph, d)
        swap(i).start()

        @pl.when(i > 0)
        def _():
            swap_add(i - 1)

        @pl.when(i == 0)
        def _():
            arrive(yc)
            for copy in yc2:
                copy.start()
            late[0].start()
            late[1].start()

        @pl.when(i == 4)
        def _():
            for copy in pa1:
                copy.start()

        @pl.when(i == 5)
        def _():
            arrive(ya2)
            arrive(yb2)
            arrive(yc2)
            late[2].start()

    swap_add(7)
    pb1 = p_send1(1)
    arrive(shared)
    pa2, pb2 = p_send2(0, False), p_send2(1, False)

    @pl.loop(0, 8)
    def _(i):
        backward(i, q, qr, og, k, g, ph, dk, dr)

        @pl.when(i == 0)
        def _():
            arrive(pa1)
            p_add1(0)
            for copy in pa2:
                copy.start()

        @pl.when(i == 2)
        def _():
            arrive(pb1)
            p_add1(1)
            for copy in pb2:
                copy.start()

        @pl.when(i == 6)
        def _():
            arrive(pa2)
            p_add2(0)

    links.finish()
    links.started = []
    for n in range(2):
        for j in range(SEL):
            fold = dr[n, 64 * j : 64 * j + 64, :]
            fold = fold[:, :64] + fold[:, 64:]
            drp[SEL * n + j] = jnp.concatenate([fold[:32], fold[32:]], axis=1)

    def fill(o):
        hits = [
            [jnp.where(ids[n, j] == o * 3 + part, 1.0, 0.0).astype(F32) for n in range(2) for j in range(SEL)]
            for part in range(3)
        ]
        packs = []
        for part in range(3):
            pack = jnp.zeros((32, 128), F32)
            for n in range(2 * SEL):
                pack = pack + hits[part][n] * drp[n]
            packs.append(pack.astype(BF))
            for r in range(4):
                total = jnp.zeros((16, LAT), F32)
                for n in range(2 * SEL):
                    low = 64 * (n % SEL) + 16 * r
                    total = total + hits[part][n] * dk[n // SEL, low : low + 16, :]
                kc[o, 4 * part + r] = total.astype(BF)
        packs = jnp.concatenate(packs + [jnp.zeros((32, 128), BF)], axis=1)
        kc[o, 12] = packs[:16]
        kc[o, 13] = packs[16:]

    def away(o, slot, way, side=0, rows=None):
        src, dst = kc.at[o], cin.at[slot]
        if rows is not None:
            src, dst = src.at[rows], dst.at[rows]
        return links.push(src, dst, way, side)

    def take(o, slots, rows=slice(None)):
        total = kc[o, rows].astype(F32)
        for slot in slots:
            total = total + cin[slot, rows].astype(F32)
        kc[o, rows] = total.astype(BF)

    lower, higher = slice(0, HALF), slice(HALF, TILES)
    fill(oth(4))
    cross4 = away(oth(4), 0, "far")
    fill(oth(3))
    fill(oth(-3))
    third = [away(oth(3), 1, "z", 0), away(oth(-3), 2, "z", 1)]
    fill(oth(2))
    fill(oth(-2))
    fill(own(4))
    arrive(pb2)
    p_add2(1)
    w = q_send1()
    arrive(third)
    take(oth(2), [1])
    take(oth(-2), [2])
    cross2 = [away(oth(2), 3, "far"), away(oth(-2), 4, "far")]
    arrive([cross4])
    take(own(4), [0])
    c = [away(own(4), 5, "z", 0, upper(0)), away(own(4), 6, "z", 1, upper(1))]
    fill(own(3))
    fill(own(-3))
    arrive(w)
    q_add1()
    w = q_send2()
    arrive(c)
    take(own(3), [5], lower)
    take(own(-3), [6], higher)
    c = [away(own(3), 7, "z", 0), away(own(-3), 8, "z", 1)]
    fill(oth(1))
    fill(oth(-1))
    near = [away(oth(1), 9, "z", 0, upper(1)), away(oth(-1), 10, "z", 1, upper(0))]
    cross1 = [away(oth(1), 11, "far", 0, upper(0)), away(oth(-1), 12, "far", 0, upper(1))]
    fill(own(2))
    fill(own(-2))
    fill(oth(0))
    arrive(w)
    q_add2()
    w = [
        links.push(
            d.at[part, core, mine[part], mine[1 - part], (z + n) % 8], zin.at[part, n - 1], ("z", n)
        )
        for n in (4, 3, 5, 2, 6, 1, 7)
        for part in (0, 1)
    ]
    arrive(c)
    arrive(cross2)
    take(own(2), [7, 3])
    take(own(-2), [8, 4])
    c = [away(own(2), 13, "z", 0), away(own(-2), 14, "z", 1)]
    arrive(near)
    take(oth(0), [9], higher)
    take(oth(0), [10], lower)
    cross0 = away(oth(0), 15, "far")
    fill(own(1))
    fill(own(-1))
    fill(own(0))
    arrive(cross1)
    take(own(1), [11], lower)
    take(own(-1), [12], higher)
    arrive(c)
    take(own(1), [13])
    take(own(-1), [14])
    c = [away(own(1), 16, "z", 0), away(own(-1), 17, "z", 1)]
    arrive(w)
    wg[0:64, :] = total_of(0)
    wg[64:128, :] = total_of(1)
    arrive([cross0])
    arrive(c)
    total = kc[own(0)].astype(F32)
    for slot in (15, 16, 17):
        total = total + cin[slot].astype(F32)
    cg[...] = total[0:12].astype(BF)
    pack = total[12:14].reshape(32, LAT)
    rows = [pack[:, 64 * i : 64 * i + 64] for i in range(6)] + [jnp.zeros((64, ROPE), F32)]
    flipped = jnp.concatenate(rows, axis=0)
    flipped = jnp.concatenate([flipped, jnp.zeros((256, 128 - ROPE), F32)], axis=1).T
    rg[...] = flipped[:ROPE, :192].astype(BF)
    links.finish()

    @pl.loop(0, 8)
    def _(i):
        swap(i).wait_send()


def run(ids, counts, cache, rope, weight, q, qr, og):
    return pl.pallas_call(
        core_kernel,
        out_shape=(
            jax.ShapeDtypeStruct((12, 16, LAT), BF),
            jax.ShapeDtypeStruct((ROPE, 192), BF),
            jax.ShapeDtypeStruct((128, HD), F32),
        ),
        in_specs=[pl.BlockSpec(memory_space=pltpu.SMEM)] * 2 + [pl.BlockSpec(memory_space=pl.ANY)] * 6,
        out_specs=(pl.BlockSpec(memory_space=pltpu.VMEM),) * 3,
        scratch_shapes=[
            pltpu.VMEM((16, TILES, 16, LAT), BF),
            pltpu.VMEM((2, 4, 4, 8, 128, HD), BF),
            pltpu.VMEM((2, 2, 4, 4, 8, 64, HD), BF),
            pltpu.VMEM((2, 4, 4, 8, 64, HD), BF),
            pltpu.VMEM((128, 64 * LAT), BF),
            pltpu.VMEM((128, 64 * ROPE), BF),
            pltpu.VMEM((128, 64 * HD), BF),
            pltpu.VMEM((ROPE, 192), BF),
            pltpu.VMEM((2, 256, LAT + 128), BF),
            pltpu.VMEM((2, LAT, 256), BF),
            pltpu.VMEM((2, 256, 128), F32),
            pltpu.VMEM((8, 2, 256, 512), BF),
            pltpu.VMEM((2, 256, LAT), F32),
            pltpu.VMEM((2, 256, 128), F32),
            pltpu.VMEM((2 * SEL, 32, 128), F32),
            pltpu.VMEM((18, TILES, 16, LAT), BF),
            pltpu.VMEM((2, 2, 2, 2, 4, 64, HD), BF),
            pltpu.VMEM((2, 2, 2, 4, 4, 64, HD), BF),
            pltpu.VMEM((2, 2, 4, 64, HD), BF),
            pltpu.VMEM((2, 2, 8, 64, HD), BF),
            pltpu.VMEM((2, 7, 64, HD), BF),
            pltpu.SemaphoreType.DMA((130,)),
            pltpu.SemaphoreType.DMA((130,)),
            pltpu.SemaphoreType.DMA((7,)),
        ],
        compiler_params=pltpu.CompilerParams(
            collective_id=0, has_side_effects=True, vmem_limit_bytes=63 * 2**20
        ),
        name="whole",
    )(ids, counts, cache, rope, weight, q, qr, og)


def shards(
    q_latent,
    q_rope,
    latent_cache,
    rope_keys,
    up_weight,
    out_grad,
    block_ids,
    block_counts,
    slab_offset,
):
    cg, rg, wg = run(
        block_ids[0],
        block_counts[0],
        latent_cache.reshape(12, 16, LAT),
        rope_keys[0].T,
        up_weight.reshape(128, HD),
        q_latent[0],
        q_rope[0],
        out_grad[0],
    )
    return cg.reshape(1, 192, LAT), rg.T[None], wg.reshape(4, 32, HD)


def solution(mesh):
    placed = (
        P("dp", "ctx", None),
        P("dp", "ctx", None),
        P("dp", "ctx", None),
        P("dp", "ctx", None),
        P("ctx", "dp", None),
        P("dp", "ctx", None),
        P("dp", "ctx", None),
        P("dp", "ctx"),
        P("dp"),
    )
    return jax.shard_map(
        shards,
        mesh=mesh,
        in_specs=placed,
        out_specs=(P("dp", "ctx", None), P("dp", "ctx", None), P("ctx", "dp", None)),
        check_vma=False,
    )
```

time: 1040 us -> 144 us (0.14)
  waiting for transfers between devices: 541 us -> 0 us
  blocking collectives: 250 us -> 0 us
  Pallas kernels: 0 us -> 138 us
  local copies, waits for them, and re-layouts: 119 us -> 4.46 us
  matrix products: 62 us -> 0 us
  starting transfers between devices: 24 us -> 0 us
  other arithmetic: 20.5 us -> 0 us
  between operations: 14.8 us -> 0.64 us
    reduce_scatter x3 -> x0, waiting for transfers between devices: 376 us -> none  [the longest x1 225 us: shards(): lax.psum_scatter(dense_key, 'ctx', scatter_dimension=0, tiled=True)]
    all_gather x2 -> x0, blocking collectives: 250 us -> none  [the longest x1 230 us: shards(): lax.all_gather(rope_keys[0], 'ctx', axis=0, tiled=True)]
    all_to_all x3 -> x0, waiting for transfers between devices: 164 us -> none  [the longest x1 133 us: shards(): lax.all_to_all(out_latent, 'ctx', split_axis=1, concat_axis=0, tiled=True)]
    pallas_call x0 -> x1, Pallas kernels: none -> 138 us  [run(): pl.pallas_call(core_kernel, out_shape=(jax.ShapeDtypeStruct((12, 16, LAT)...]
    dot_general x8 -> x0, matrix products: 54.5 us -> none  [the longest x1 9.04 us: attend(): jnp.einsum('bthl,bkl->bthk', q_tiles, key_tiles, preferred_element_type=j...]
    all_to_all x5 -> x0, local copies, waits for them, and re-layouts: 51.7 us -> none  [the longest x2 25.3 us: shards(): lax.all_to_all(out_latent, 'ctx', split_axis=1, concat_axis=0, tiled=True)]
    reshape x4 -> x0, local copies, waits for them, and re-layouts: 32 us -> none  [the longest x1 14.7 us: project(): latent_rows = out_latent.reshape(-1, head_count, LAT)]
    all_to_all x3 -> x0, starting transfers between devices: 23.7 us -> none  [the longest x1 11 us: shards(): lax.all_to_all(out_grad[0], 'ctx', split_axis=1, concat_axis=0, tiled=True)]
  transfers between devices with their start and end apart: 7 -> 0, of which waited for: 5 -> 0; matrix products, arithmetic and copies ran while one was open for 14% -> 0% of each run, Pallas kernels for 0% -> 0%
where the time goes in v2:
time: 144 us
  Pallas kernels  138 us (96%)
  local copies, waits for them, and re-layouts  4.46 us (3%)
    pallas_call x1, Pallas kernels, run(): pl.pallas_call(core_kernel, out_shape=(jax.ShapeDtypeStruct((12, 16, LAT)...  138 us
    unnamed x3, local copies, waits for them, and re-layouts  4.46 us

profile of v2, /device:TPU:8, one launch (start us, length us, event | category | flops | bytes accessed | tf_op | source)
XLA Modules:
  0.0 143.5 jit_solution(10020991847363932050)
XLA Ops:
  0.6 138.4 %whole.1 = (bf16[12,16,512]{2,1,0:T(8,128)(2,1)}, bf16[64,192]{1,0:T(8,128)(2,1)}, f32[128,128]{1,0:T(8,128)}) custom-call(s32[2,4]{1,0:T(2,128)} %bitcast.24, s32[2]{0:T(128)} %bitcast.25, bf16[12,16,512]{2,1,0:T(8,128)(2,1)} %bitcast.19, bf16[64,192]{1,0:T(8,128)(2,1)} %bitcast.21, bf16[128,128]{1,0:T(8,128)(2,1)} %bitcast.22, ...), custom_call_target="tpu_custom_call" | custom-call | tf_op jit(solution)/shard_map/whole/pallas_call | solution.py:597
  139.1 1.6 %copy.14 = bf16[1,192,512]{2,1,0:T(8,128)(2,1)} copy(bf16[1,192,512]{2,1,0:T(8,128)(2,1)} %bitcast.18) | data formatting | bytes 393216
  140.7 1.4 copy.15
  142.1 1.5 %copy.16 = f32[4,32,128]{2,1,0:T(8,128)} copy(f32[4,32,128]{2,1,0:T(8,128)} %bitcast.20) | data formatting | bytes 131072

commit v3 on v2

--- a/solution.py
+++ b/solution.py
@@ -263,12 +263,11 @@
     wz = [links.push(weights, weights, ("z", n)) for n in (4, 3, 5, 2, 6, 1, 7)]
     arrive(c)
     c = ring8(2)
-    cross1 = [push_block(own(1), "far", 0, upper(0)), push_block(own(-1), "far", 0, upper(1))]
     arrive(wz)
     ya = ring_y1(0)
     wx = ring_x(1)
     arrive([cross0])
-    near = [push_block(oth(0), "z", 0, upper(0)), push_block(oth(0), "z", 1, upper(1))]
+    near = [push_block(oth(0), "z", 0), push_block(oth(0), "z", 1)]
     arrive(c)
     c = ring8(3)
     cross2 = [push_block(own(2), "far"), push_block(own(-2), "far")]
@@ -299,7 +298,6 @@
     dr[...] = jnp.zeros_like(dr)
     for copy in loads:
         copy.wait()
-    arrive(cross1)
     arrive(near)
     arrive([cross4])
     arrive(third)
@@ -530,13 +528,13 @@
     c = [away(own(4), 5, "z", 0, upper(0)), away(own(4), 6, "z", 1, upper(1))]
     fill(own(3))
     fill(own(-3))
-    arrive(w)
-    q_add1()
-    w = q_send2()
     arrive(c)
     take(own(3), [5], lower)
     take(own(-3), [6], higher)
     c = [away(own(3), 7, "z", 0), away(own(-3), 8, "z", 1)]
+    arrive(w)
+    q_add1()
+    w = q_send2()
     fill(oth(1))
     fill(oth(-1))
     near = [away(oth(1), 9, "z", 0, upper(1)), away(oth(-1), 10, "z", 1, upper(0))]
@@ -544,6 +542,15 @@
     fill(own(2))
     fill(own(-2))
     fill(oth(0))
+    arrive(c)
+    arrive(cross2)
+    take(own(2), [7, 3])
+    take(own(-2), [8, 4])
+    c = [away(own(2), 13, "z", 0), away(own(-2), 14, "z", 1)]
+    arrive(near)
+    take(oth(0), [9], higher)
+    take(oth(0), [10], lower)
+    cross0 = away(oth(0), 15, "far")
     arrive(w)
     q_add2()
     w = [
@@ -553,15 +560,6 @@
         for n in (4, 3, 5, 2, 6, 1, 7)
         for part in (0, 1)
     ]
-    arrive(c)
-    arrive(cross2)
-    take(own(2), [7, 3])
-    take(own(-2), [8, 4])
-    c = [away(own(2), 13, "z", 0), away(own(-2), 14, "z", 1)]
-    arrive(near)
-    take(oth(0), [9], higher)
-    take(oth(0), [10], lower)
-    cross0 = away(oth(0), 15, "far")
     fill(own(1))
     fill(own(-1))
     fill(own(0))
@@ -591,6 +589,27 @@
     @pl.loop(0, 8)
     def _(i):
         swap(i).wait_send()
+
+
+def finish_kernel(cg, rg, wg, cg_out, rg_out, wg_out, sem):
+    pairs = ((cg, cg_out), (rg, rg_out), (wg, wg_out))
+    copies = [pltpu.make_async_copy(src, dst, sem.at[n]) for n, (src, dst) in enumerate(pairs)]
+    for copy in copies:
+        copy.start()
+    for copy in copies:
+        copy.wait()
+
+
+def finish(*arrays):
+    return pl.pallas_call(
+        finish_kernel,
+        out_shape=tuple(jax.ShapeDtypeStruct(a.shape, a.dtype) for a in arrays),
+        in_specs=[pl.BlockSpec(memory_space=pl.ANY)] * 3,
+        out_specs=(pl.BlockSpec(memory_space=pl.ANY),) * 3,
+        scratch_shapes=[pltpu.SemaphoreType.DMA((3,))],
+        compiler_params=pltpu.CompilerParams(vmem_limit_bytes=63 * 2**20),
+        name="finish",
+    )(*arrays)
 
 
 def run(ids, counts, cache, rope, weight, q, qr, og):
@@ -647,7 +666,7 @@
     block_counts,
     slab_offset,
 ):
-    cg, rg, wg = run(
+    cg, rg, wg = finish(*run(
         block_ids[0],
         block_counts[0],
         latent_cache.reshape(12, 16, LAT),
@@ -656,7 +675,7 @@
         q_latent[0],
         q_rope[0],
         out_grad[0],
-    )
+    ))
     return cg.reshape(1, 192, LAT), rg.T[None], wg.reshape(4, 32, HD)
 
 

time: 144 us -> 142 us (0.986)
  local copies, waits for them, and re-layouts: 4.46 us -> 0 us
  Pallas kernels: 138 us -> 141 us
    pallas_call x0 -> x1, Pallas kernels: none -> 10.1 us  [finish(): pl.pallas_call(finish_kernel, out_shape=tuple((jax.ShapeDtypeStruct(a.sha...]
    pallas_call x1, Pallas kernels: 138 us -> 131 us  [run(): pl.pallas_call(core_kernel, out_shape=(jax.ShapeDtypeStruct((12, 16, LAT)...]
    unnamed x3 -> x0, local copies, waits for them, and re-layouts: 4.46 us -> none
where the time goes in v3:
time: 142 us
  Pallas kernels  141 us (99%)
    pallas_call x1, Pallas kernels, run(): pl.pallas_call(core_kernel, out_shape=(jax.ShapeDtypeStruct((12, 16, LAT)...  131 us
    pallas_call x1, Pallas kernels, finish(): pl.pallas_call(finish_kernel, out_shape=tuple((jax.ShapeDtypeStruct(a.sha...  10.1 us

profile of v3, /device:TPU:8, one launch (start us, length us, event | category | flops | bytes accessed | tf_op | source)
XLA Modules:
  0.0 141.9 jit_solution(8832010398081990201)
XLA Ops:
  0.6 131.2 %whole.1 = (bf16[12,16,512]{2,1,0:T(8,128)(2,1)}, bf16[64,192]{1,0:T(8,128)(2,1)}, f32[128,128]{1,0:T(8,128)}) custom-call(s32[2,4]{1,0:T(2,128)} %bitcast.21, s32[2]{0:T(128)} %bitcast.22, bf16[12,16,512]{2,1,0:T(8,128)(2,1)} %bitcast.18, bf16[64,192]{1,0:T(8,128)(2,1)} %bitcast.19, bf16[128,128]{1,0:T(8,128)(2,1)} %bitcast.20, ...), custom_call_target="tpu_custom_call" | custom-call | tf_op jit(solution)/shard_map/whole/pallas_call | solution.py:616
  131.9 10.1 %finish.1 = (bf16[12,16,512]{2,1,0:T(8,128)(2,1)}, bf16[64,192]{1,0:T(8,128)(2,1)}, f32[128,128]{1,0:T(8,128)}) custom-call(bf16[12,16,512]{2,1,0:T(8,128)(2,1)} %get-tuple-element.9.cg, bf16[64,192]{1,0:T(8,128)(2,1)} %get-tuple-element.10.rg, f32[128,128]{1,0:T(8,128)} %get-tuple-element.11.wg), custom_call_target="tpu_custom_call" | custom-call | tf_op jit(solution)/shard_map/finish/pallas_call | solution.py:604

commit v4 on v3

--- a/solution.py
+++ b/solution.py
@@ -133,15 +133,16 @@
     return jnp.concatenate(parts, axis=0)
 
 
-def forward(i, q, qr, og, k, kt, bias, ph, d):
-    outs = []
+def scores(i, q, qr, k, bias, ph):
     for b in range(2):
         qs = jnp.concatenate([queries(q, i, b), rotary(qr, i, b)], axis=1)
         s = dot(k[b], qs, NT) * SCALE + jnp.concatenate([bias[b]] * 4, axis=1)
         e = jnp.exp(s - jnp.max(s, axis=0, keepdims=True))
-        half = (e * (1.0 / jnp.sum(e, axis=0, keepdims=True))).astype(BF)
-        ph[i, b] = half
-        outs.append(dot(kt[b], half, NN).astype(BF))
+        ph[i, b] = (e * (1.0 / jnp.sum(e, axis=0, keepdims=True))).astype(BF)
+
+
+def outputs(i, og, kt, ph, d):
+    outs = [dot(kt[b], ph[i, b], NN).astype(BF) for b in range(2)]
     for pair in range(4):
         xh, part = pair // 2, pair % 2
         both = jnp.concatenate([out[:, 128 * pair : 128 * pair + 128] for out in outs], axis=1)
@@ -409,16 +410,19 @@
     late = [share(1, False), share(3, False), share(2, False)]
     pa1 = p_send1(0, False)
 
-    @pl.loop(0, 8)
+    scores(0, q, qr, k, bias, ph)
+
+    @pl.loop(1, 8)
     def _(i):
-        forward(i, q, qr, og, k, kt, bias, ph, d)
-        swap(i).start()
-
-        @pl.when(i > 0)
+        scores(i, q, qr, k, bias, ph)
+        outputs(i - 1, og, kt, ph, d)
+        swap(i - 1).start()
+
+        @pl.when(i > 1)
         def _():
-            swap_add(i - 1)
-
-        @pl.when(i == 0)
+            swap_add(i - 2)
+
+        @pl.when(i == 1)
         def _():
             arrive(yc)
             for copy in yc2:
@@ -426,18 +430,21 @@
             late[0].start()
             late[1].start()
 
-        @pl.when(i == 4)
+        @pl.when(i == 5)
         def _():
             for copy in pa1:
                 copy.start()
 
-        @pl.when(i == 5)
+        @pl.when(i == 6)
         def _():
             arrive(ya2)
             arrive(yb2)
             arrive(yc2)
             late[2].start()
 
+    outputs(7, og, kt, ph, d)
+    swap(7).start()
+    swap_add(6)
     swap_add(7)
     pb1 = p_send1(1)
     arrive(shared)
@@ -591,23 +598,18 @@
         swap(i).wait_send()
 
 
-def finish_kernel(cg, rg, wg, cg_out, rg_out, wg_out, sem):
-    pairs = ((cg, cg_out), (rg, rg_out), (wg, wg_out))
-    copies = [pltpu.make_async_copy(src, dst, sem.at[n]) for n, (src, dst) in enumerate(pairs)]
-    for copy in copies:
-        copy.start()
-    for copy in copies:
-        copy.wait()
+def finish_kernel(cg, rg, wg, cg_out, rg_out, wg_out):
+    cg_out[...] = cg[...]
+    rg_out[...] = rg[...]
+    wg_out[...] = wg[...]
 
 
 def finish(*arrays):
     return pl.pallas_call(
         finish_kernel,
         out_shape=tuple(jax.ShapeDtypeStruct(a.shape, a.dtype) for a in arrays),
-        in_specs=[pl.BlockSpec(memory_space=pl.ANY)] * 3,
-        out_specs=(pl.BlockSpec(memory_space=pl.ANY),) * 3,
-        scratch_shapes=[pltpu.SemaphoreType.DMA((3,))],
-        compiler_params=pltpu.CompilerParams(vmem_limit_bytes=63 * 2**20),
+        in_specs=[pl.BlockSpec(memory_space=pltpu.VMEM)] * 3,
+        out_specs=(pl.BlockSpec(memory_space=pltpu.VMEM),) * 3,
         name="finish",
     )(*arrays)
 

time: 142 us -> 132 us (0.930)
  Pallas kernels: 141 us -> 131 us
    pallas_call x1, Pallas kernels: 10.1 us -> 1.67 us  [finish(): pl.pallas_call(finish_kernel, out_shape=tuple((jax.ShapeDtypeStruct(a.sha...]
    pallas_call x1, Pallas kernels: 131 us -> 129 us  [run(): pl.pallas_call(core_kernel, out_shape=(jax.ShapeDtypeStruct((12, 16, LAT)...]
where the time goes in v4:
time: 132 us; the launch traced here: 131 us
  Pallas kernels  131 us (99%)
    pallas_call x1, Pallas kernels, run(): pl.pallas_call(core_kernel, out_shape=(jax.ShapeDtypeStruct((12, 16, LAT)...  129 us

profile of v4, /device:TPU:8, one launch (start us, length us, event | category | flops | bytes accessed | tf_op | source)
XLA Modules:
  0.0 131.3 jit_solution(14920692886324850003)
XLA Ops:
  0.6 129.0 %whole.1 = (bf16[12,16,512]{2,1,0:T(8,128)(2,1)}, bf16[64,192]{1,0:T(8,128)(2,1)}, f32[128,128]{1,0:T(8,128)}) custom-call(s32[2,4]{1,0:T(2,128)} %bitcast.21, s32[2]{0:T(128)} %bitcast.22, bf16[12,16,512]{2,1,0:T(8,128)(2,1)} %bitcast.18, bf16[64,192]{1,0:T(8,128)(2,1)} %bitcast.19, bf16[128,128]{1,0:T(8,128)(2,1)} %bitcast.20, ...), custom_call_target="tpu_custom_call" | custom-call | tf_op jit(solution)/shard_map/whole/pallas_call | solution.py:618
  129.7 1.7 %finish.1 = (bf16[12,16,512]{2,1,0:T(8,128)(2,1)}, bf16[64,192]{1,0:T(8,128)(2,1)}, f32[128,128]{1,0:T(8,128)}) custom-call(bf16[12,16,512]{2,1,0:T(8,128)(2,1)} %get-tuple-element.9.cg, bf16[64,192]{1,0:T(8,128)(2,1)} %get-tuple-element.10.rg, f32[128,128]{1,0:T(8,128)} %get-tuple-element.11.wg), custom_call_target="tpu_custom_call" | custom-call | tf_op jit(solution)/shard_map/finish/pallas_call | solution.py:608

commit v5 on v4

--- a/solution.py
+++ b/solution.py
@@ -203,7 +203,7 @@
         pltpu.make_async_copy(og_hbm, og, lsem.at[5]),
         pltpu.make_async_copy(q_hbm, q, lsem.at[6]),
     ]
-    for copy in first + loads:
+    for copy in first:
         copy.start()
     links.barrier()
     for copy in first:
@@ -243,6 +243,11 @@
         shared.append(links.push(ref, ref, "core", 0, start))
         return shared[-1]
 
+    def share_far(n):
+        ref = g.at[core, (y + 2) % 4, (x + n) % 4]
+        shared.append(links.push(ref, ref, "core", 0, False))
+        return shared[-1]
+
     def ring8(s):
         out = []
         for side, sign in ((0, 1), (1, -1)):
@@ -264,6 +269,8 @@
     wz = [links.push(weights, weights, ("z", n)) for n in (4, 3, 5, 2, 6, 1, 7)]
     arrive(c)
     c = ring8(2)
+    for copy in loads:
+        copy.start()
     arrive(wz)
     ya = ring_y1(0)
     wx = ring_x(1)
@@ -407,7 +414,7 @@
         return total
 
     yc2 = ring_y2(2, False)
-    late = [share(1, False), share(3, False), share(2, False)]
+    late = [share(1, False), share(3, False)] + [share_far(n) for n in (0, 1, 3, 2)]
     pa1 = p_send1(0, False)
 
     scores(0, q, qr, k, bias, ph)
@@ -427,24 +434,26 @@
             arrive(yc)
             for copy in yc2:
                 copy.start()
-            late[0].start()
-            late[1].start()
+            arrive(ya2)
+            for copy in late[:3]:
+                copy.start()
 
         @pl.when(i == 5)
         def _():
             for copy in pa1:
                 copy.start()
 
-        @pl.when(i == 6)
+        @pl.when(i == 4)
         def _():
-            arrive(ya2)
             arrive(yb2)
-            arrive(yc2)
-            late[2].start()
+            late[3].start()
+            late[4].start()
 
     outputs(7, og, kt, ph, d)
     swap(7).start()
     swap_add(6)
+    arrive(yc2)
+    late[5].start()
     swap_add(7)
     pb1 = p_send1(1)
     arrive(shared)

time: 132 us -> 132 us (level)
  no operation moved by 1% of the time
where the time goes in v5:
time: 132 us
  Pallas kernels  131 us (99%)
    pallas_call x1, Pallas kernels, run(): pl.pallas_call(core_kernel, out_shape=(jax.ShapeDtypeStruct((12, 16, LAT)...  130 us

profile of v5, /device:TPU:8, one launch (start us, length us, event | category | flops | bytes accessed | tf_op | source)
XLA Modules:
  0.0 131.8 jit_solution(718903460721174275)
XLA Ops:
  0.6 129.5 %whole.1 = (bf16[12,16,512]{2,1,0:T(8,128)(2,1)}, bf16[64,192]{1,0:T(8,128)(2,1)}, f32[128,128]{1,0:T(8,128)}) custom-call(s32[2,4]{1,0:T(2,128)} %bitcast.21, s32[2]{0:T(128)} %bitcast.22, bf16[12,16,512]{2,1,0:T(8,128)(2,1)} %bitcast.18, bf16[64,192]{1,0:T(8,128)(2,1)} %bitcast.19, bf16[128,128]{1,0:T(8,128)(2,1)} %bitcast.20, ...), custom_call_target="tpu_custom_call" | custom-call | tf_op jit(solution)/shard_map/whole/pallas_call | solution.py:627
  130.1 1.7 %finish.1 = (bf16[12,16,512]{2,1,0:T(8,128)(2,1)}, bf16[64,192]{1,0:T(8,128)(2,1)}, f32[128,128]{1,0:T(8,128)}) custom-call(bf16[12,16,512]{2,1,0:T(8,128)(2,1)} %get-tuple-element.9.cg, bf16[64,192]{1,0:T(8,128)(2,1)} %get-tuple-element.10.rg, f32[128,128]{1,0:T(8,128)} %get-tuple-element.11.wg), custom_call_target="tpu_custom_call" | custom-call | tf_op jit(solution)/shard_map/finish/pallas_call | solution.py:617

commit v6 on v5

--- a/solution.py
+++ b/solution.py
@@ -248,20 +248,21 @@
         shared.append(links.push(ref, ref, "core", 0, False))
         return shared[-1]
 
+    kept = []
+
     def ring8(s):
         out = []
         for side, sign in ((0, 1), (1, -1)):
-            ref = kc.at[own(-sign * (s - 1))]
-            if s == 4:
-                ref = ref.at[upper(side)]
-            out.append(links.push(ref, ref, "z", side))
+            rows = upper(side) if s == 4 else None
+            out.append(push_block(own(-sign * (s - 1)), "z", side, rows))
         return out
 
     def push_block(o, way, side=0, rows=None):
         ref = kc.at[o]
         if rows is not None:
             ref = ref.at[rows]
-        return links.push(ref, ref, way, side)
+        kept.append(links.push(ref, ref, way, side))
+        return kept[-1]
 
     weights = g.at[core, y, x, z]
     c = ring8(1)
@@ -482,8 +483,9 @@
             arrive(pa2)
             p_add2(0)
 
-    links.finish()
-    links.started = []
+    for copy in kept:
+        copy.wait_send()
+    links.started = [copy for copy in links.started if not any(copy is other for other in kept)]
     for n in range(2):
         for j in range(SEL):
             fold = dr[n, 64 * j : 64 * j + 64, :]
@@ -554,10 +556,10 @@
     fill(oth(1))
     fill(oth(-1))
     near = [away(oth(1), 9, "z", 0, upper(1)), away(oth(-1), 10, "z", 1, upper(0))]
-    cross1 = [away(oth(1), 11, "far", 0, upper(0)), away(oth(-1), 12, "far", 0, upper(1))]
     fill(own(2))
     fill(own(-2))
     fill(oth(0))
+    cross1 = [away(oth(1), 11, "far", 0, upper(0)), away(oth(-1), 12, "far", 0, upper(1))]
     arrive(c)
     arrive(cross2)
     take(own(2), [7, 3])

time: 132 us -> 135 us (1.023); the launches traced: 132 us -> 133 us
  no operation moved by 1% of the time
where the time goes in v6:
time: 135 us; the launch traced here: 133 us
  Pallas kernels  132 us (98%)
    pallas_call x1, Pallas kernels, run(): pl.pallas_call(core_kernel, out_shape=(jax.ShapeDtypeStruct((12, 16, LAT)...  131 us

profile of v6, /device:TPU:8, one launch (start us, length us, event | category | flops | bytes accessed | tf_op | source)
XLA Modules:
  0.0 132.8 jit_solution(11685688432333012229)
XLA Ops:
  0.6 130.5 %whole.1 = (bf16[12,16,512]{2,1,0:T(8,128)(2,1)}, bf16[64,192]{1,0:T(8,128)(2,1)}, f32[128,128]{1,0:T(8,128)}) custom-call(s32[2,4]{1,0:T(2,128)} %bitcast.21, s32[2]{0:T(128)} %bitcast.22, bf16[12,16,512]{2,1,0:T(8,128)(2,1)} %bitcast.18, bf16[64,192]{1,0:T(8,128)(2,1)} %bitcast.19, bf16[128,128]{1,0:T(8,128)(2,1)} %bitcast.20, ...), custom_call_target="tpu_custom_call" | custom-call | tf_op jit(solution)/shard_map/whole/pallas_call | solution.py:629
  131.2 1.7 %finish.1 = (bf16[12,16,512]{2,1,0:T(8,128)(2,1)}, bf16[64,192]{1,0:T(8,128)(2,1)}, f32[128,128]{1,0:T(8,128)}) custom-call(bf16[12,16,512]{2,1,0:T(8,128)(2,1)} %get-tuple-element.9.cg, bf16[64,192]{1,0:T(8,128)(2,1)} %get-tuple-element.10.rg, f32[128,128]{1,0:T(8,128)} %get-tuple-element.11.wg), custom_call_target="tpu_custom_call" | custom-call | tf_op jit(solution)/shard_map/finish/pallas_call | solution.py:619

commit v7 on v5

--- a/solution.py
+++ b/solution.py
@@ -554,10 +554,10 @@
     fill(oth(1))
     fill(oth(-1))
     near = [away(oth(1), 9, "z", 0, upper(1)), away(oth(-1), 10, "z", 1, upper(0))]
-    cross1 = [away(oth(1), 11, "far", 0, upper(0)), away(oth(-1), 12, "far", 0, upper(1))]
     fill(own(2))
     fill(own(-2))
     fill(oth(0))
+    cross1 = [away(oth(1), 11, "far", 0, upper(0)), away(oth(-1), 12, "far", 0, upper(1))]
     arrive(c)
     arrive(cross2)
     take(own(2), [7, 3])

time: 132 us -> 132 us (level)
  no operation moved by 1% of the time
where the time goes in v7:
time: 132 us
  Pallas kernels  131 us (99%)
    pallas_call x1, Pallas kernels, run(): pl.pallas_call(core_kernel, out_shape=(jax.ShapeDtypeStruct((12, 16, LAT)...  130 us

profile of v7, /device:TPU:8, one launch (start us, length us, event | category | flops | bytes accessed | tf_op | source)
XLA Modules:
  0.0 131.8 jit_solution(14142701236865919923)
XLA Ops:
  0.6 129.5 %whole.1 = (bf16[12,16,512]{2,1,0:T(8,128)(2,1)}, bf16[64,192]{1,0:T(8,128)(2,1)}, f32[128,128]{1,0:T(8,128)}) custom-call(s32[2,4]{1,0:T(2,128)} %bitcast.21, s32[2]{0:T(128)} %bitcast.22, bf16[12,16,512]{2,1,0:T(8,128)(2,1)} %bitcast.18, bf16[64,192]{1,0:T(8,128)(2,1)} %bitcast.19, bf16[128,128]{1,0:T(8,128)(2,1)} %bitcast.20, ...), custom_call_target="tpu_custom_call" | custom-call | tf_op jit(solution)/shard_map/whole/pallas_call | solution.py:627
  130.1 1.7 %finish.1 = (bf16[12,16,512]{2,1,0:T(8,128)(2,1)}, bf16[64,192]{1,0:T(8,128)(2,1)}, f32[128,128]{1,0:T(8,128)}) custom-call(bf16[12,16,512]{2,1,0:T(8,128)(2,1)} %get-tuple-element.9.cg, bf16[64,192]{1,0:T(8,128)(2,1)} %get-tuple-element.10.rg, f32[128,128]{1,0:T(8,128)} %get-tuple-element.11.wg), custom_call_target="tpu_custom_call" | custom-call | tf_op jit(solution)/shard_map/finish/pallas_call | solution.py:617
